TPU v7x, 128 devices: a whole 4x4x4 slice. The times are simulated.
128 devices in a mesh: section: 2 (over x_hi), group: 16 (over z, y), replica: 4 (over x_lo, core).
Axes of the slice: x: 4 (x_hi: 2, x_lo: 2; x = x_hi * 2 + x_lo), y: 4, z: 4, core: 2. Of those that a mesh axis runs over, the one named last changes fastest.
Arguments:
- inputs: bfloat16 [4, 2, 1024, 896], P('replica', None, 'group'), may hold values from -6 to 6
- cotangent: bfloat16 [4, 2, 1024, 896], P('replica', None, 'group'), may hold values from -6 to 6
- segments: int32 [4, 2048], P('replica'), may hold values from 0 to 6, as said below
- w_qkv: bfloat16 [2, 896, 1152], P('section', 'group'), may hold values from -0.1875 to 0.1875
- b_qkv: bfloat16 [2, 1152], P('section', 'group'), may hold values from -3 to 3
- w_out: bfloat16 [2, 896, 896], P('section', 'group'), may hold values from -1.5 to 1.5
- w_gate: bfloat16 [2, 896, 4864], P('section', 'group'), may hold values from -0.1875 to 0.1875
- w_up: bfloat16 [2, 896, 4864], P('section', 'group'), may hold values from -0.1875 to 0.1875
- w_down: bfloat16 [2, 4864, 896], P('section', 'group'), may hold values from -0.15625 to 0.15625
- g_attn: bfloat16 [2, 896], P('section', 'group'), may hold values from 0.5 to 1.5
- g_mlp: bfloat16 [2, 896], P('section', 'group'), may hold values from 0.5 to 1.5
Outputs:
- block_out: bfloat16 [2, 4, 2, 1024, 896], P('section', 'replica', None, 'group')
- input_grad: bfloat16 [2, 4, 2, 1024, 896], P('section', 'replica', None, 'group')
- grad_qkv: float32 [2, 896, 1152], P('section', 'group')
- grad_bias: float32 [2, 1024], P('section', 'group')
- grad_value_bias: float32 [2, 128], P('section', 'group')
- grad_out: float32 [2, 896, 896], P('section', 'group')
- grad_gate: float32 [2, 896, 4864], P('section', 'group')
- grad_up: float32 [2, 896, 4864], P('section', 'group')
- grad_down: float32 [2, 4864, 896], P('section', 'group')
- grad_attn_gain: float32 [2, 896], P('section', 'group')
- grad_mlp_gain: float32 [2, 896], P('section', 'group')
Inputs may be any that keep to these rules, and one draw needn't show every extreme that they name: `segments`: document numbers never fall along a sequence, and the last token of every sequence carries the largest; in each sequence one document covers a whole block of 1024 tokens that starts at a multiple of 1024.
All inputs are finite; a program needn't handle non-finite values.
Results may differ from a plain program's by a relative error of at most 0.035.
Values may be sent and summed in bfloat16 or wider, within the bound.
A program may use at most 192 MiB of HBM per device.

v0:
```python
import jax
import jax.numpy as jnp
from jax import lax
from jax.sharding import PartitionSpec as P

D = 896
HEADS = 14
KV_HEADS = 2
HEAD_DIM = 64
FF = 4864


EPSILON = 1e-06
THETA = 1000000.0
NEGATIVE = -1e30


def passed_along(value, axis, steps):
    count = lax.axis_size(axis)
    leading, last = (max(0, -steps), min(count, count - steps))
    return lax.ppermute(value, axis, [(source, source + steps) for source in range(leading, last)])


def rotary(positions):
    half_dim = HEAD_DIM // 2
    steps_float = jnp.arange(half_dim, dtype=jnp.float32)
    frequency = THETA ** (-steps_float * 2.0 / HEAD_DIM)
    angles = positions.astype(jnp.float32)[:, None] * frequency[None, :]
    return (jnp.cos(angles), jnp.sin(angles))


def rotate(values, cosine, sine_table):
    half_dim = values.shape[-1] // 2
    first_half = values[..., :half_dim]
    second_half = values[..., half_dim:]
    cos_rows = cosine[:, None, :]
    sin_rows = sine_table[:, None, :]
    return jnp.concatenate(
        [
            first_half * cos_rows - second_half * sin_rows,
            second_half * cos_rows + first_half * sin_rows,
        ],
        axis=-1,
    )


def rotate_back(grads, cosine, sine_table):
    half_dim = grads.shape[-1] // 2
    first_half = grads[..., :half_dim]
    second_half = grads[..., half_dim:]
    cos_rows = cosine[:, None, :]
    sin_rows = sine_table[:, None, :]
    return jnp.concatenate(
        [
            first_half * cos_rows + second_half * sin_rows,
            second_half * cos_rows - first_half * sin_rows,
        ],
        axis=-1,
    )


def rms_forward(values, gain):
    inverse = lax.rsqrt(jnp.mean(values * values, axis=-1, keepdims=True) + EPSILON)
    return (values * inverse * gain, inverse)


def rms_backward(values, inverse, gain, grads):
    scaled = grads * gain
    grad_values = inverse * scaled - values * inverse**3 * jnp.mean(
        scaled * values, axis=-1, keepdims=True
    )
    return (grad_values, jnp.sum(grads * values * inverse, axis=(0, 1)))


def span_view(segments, span_at, group_rank, row_count, span_len):
    first_row = span_at * span_len + group_rank * row_count
    positions = first_row + jnp.arange(row_count, dtype=jnp.int32)
    query_seg = lax.dynamic_slice_in_dim(segments, first_row, row_count, 1)
    cosine, sine_table = rotary(positions)
    key_pos = jnp.arange(segments.shape[1], dtype=jnp.int32)
    allowed = (key_pos[None, None, :] <= positions[None, :, None]) & (
        segments[:, None, :] == query_seg[:, :, None]
    )
    return (cosine, sine_table, allowed[:, None, None])


def project(weights, x_span, cosine, sine_table):
    seq_count, row_count = (x_span.shape[0], x_span.shape[1])
    kv_width = KV_HEADS * HEAD_DIM
    normed_float, inverse = rms_forward(x_span.astype(jnp.float32), weights[6])
    normed = normed_float.astype(jnp.bfloat16)
    projected = (
        jnp.einsum("srd,dc->src", normed, weights[0], preferred_element_type=jnp.float32)
        + weights[1]
    )
    query_rows = rotate(
        projected[..., :D].reshape(seq_count, row_count, HEADS, HEAD_DIM), cosine, sine_table
    ).astype(jnp.bfloat16)
    key_rows = rotate(
        projected[..., D : D + kv_width].reshape(seq_count, row_count, KV_HEADS, HEAD_DIM),
        cosine,
        sine_table,
    ).astype(jnp.bfloat16)
    value_rows = (
        projected[..., D + kv_width :]
        .reshape(seq_count, row_count, KV_HEADS, HEAD_DIM)
        .astype(jnp.bfloat16)
    )
    return (inverse, normed, query_rows, key_rows, value_rows)


def project_zero(x_span, cosine, sine_table):
    seq_count, row_count = (x_span.shape[0], x_span.shape[1])
    return (
        jnp.zeros((seq_count, row_count, 1), jnp.float32),
        jnp.zeros((seq_count, row_count, D), jnp.bfloat16),
        jnp.zeros((seq_count, row_count, HEADS, HEAD_DIM), jnp.bfloat16),
        jnp.zeros((seq_count, row_count, KV_HEADS, HEAD_DIM), jnp.bfloat16),
        jnp.zeros((seq_count, row_count, KV_HEADS, HEAD_DIM), jnp.bfloat16),
    )


def attention_weights(query_rows, key_cache, allowed):
    seq_count, row_count = (query_rows.shape[0], query_rows.shape[1])
    grouped = query_rows.reshape(seq_count, row_count, KV_HEADS, HEADS // KV_HEADS, HEAD_DIM)
    scores = jnp.einsum(
        "srkgd,stkd->skgrt", grouped, key_cache, preferred_element_type=jnp.float32
    ) * HEAD_DIM ** (-0.5)
    scores = jnp.where(allowed, scores, NEGATIVE)
    highest = jnp.max(scores, axis=-1, keepdims=True)
    exponent = jnp.exp(scores - highest)
    return (grouped, exponent / jnp.sum(exponent, axis=-1, keepdims=True))


def finish(weights, x_span, context):
    branch = jnp.einsum("srd,de->sre", context, weights[2], preferred_element_type=jnp.float32)
    hidden = x_span.astype(jnp.float32) + branch
    normed_float, inverse = rms_forward(hidden, weights[7])
    normed2 = normed_float.astype(jnp.bfloat16)
    gate_value = jnp.einsum("srd,df->srf", normed2, weights[3], preferred_element_type=jnp.float32)
    upward = jnp.einsum("srd,df->srf", normed2, weights[4], preferred_element_type=jnp.float32)
    product = (jax.nn.silu(gate_value) * upward).astype(jnp.bfloat16)
    output = (
        hidden + jnp.einsum("srf,fd->srd", product, weights[5], preferred_element_type=jnp.float32)
    ).astype(jnp.bfloat16)
    return (output, hidden, inverse, normed2, gate_value, upward, product)


def rear_zero(x_span, query_rows, key_cache, value_cache, allowed):
    seq_count, row_count = (x_span.shape[0], x_span.shape[1])
    lead = (seq_count, row_count)
    return (
        jnp.zeros(lead + (D,), jnp.bfloat16),
        jnp.zeros(lead + (D,), jnp.bfloat16),
        jnp.zeros(lead + (D,), jnp.float32),
        jnp.zeros(lead + (1,), jnp.float32),
        jnp.zeros(lead + (D,), jnp.bfloat16),
        jnp.zeros(lead + (FF,), jnp.float32),
        jnp.zeros(lead + (FF,), jnp.float32),
        jnp.zeros(lead + (FF,), jnp.bfloat16),
    )


def write_rows(cache, new_rows, start_row, is_valid):
    old_rows = lax.dynamic_slice_in_dim(cache, start_row, new_rows.shape[1], 1)
    chosen = jnp.where(is_valid, new_rows, old_rows)
    return lax.dynamic_update_slice_in_dim(cache, chosen, start_row, 1)


def store(stacks, values, slot_index):
    return [
        lax.dynamic_update_index_in_dim(stack, value, slot_index, 0)
        for stack, value in zip(stacks, values)
    ]


def body(inputs, cotangent, segments, w_qkv, b_qkv, w_out, w_gate, w_up, w_down, g_attn, g_mlp):
    shards = (w_qkv[0], b_qkv[0], w_out[0], w_gate[0], w_up[0], w_down[0], g_attn[0], g_mlp[0])
    weights = (
        lax.all_gather(shards[0], "group", axis=0, tiled=True),
        lax.all_gather(shards[1], "group", axis=0, tiled=True),
        lax.all_gather(shards[2], "group", axis=0, tiled=True),
        lax.all_gather(shards[3], "group", axis=0, tiled=True),
        lax.all_gather(shards[4], "group", axis=0, tiled=True),
        lax.all_gather(shards[5], "group", axis=0, tiled=True),
        lax.all_gather(shards[6], "group", axis=0, tiled=True),
        lax.all_gather(shards[7], "group", axis=0, tiled=True),
    )
    section_rank = lax.axis_index("section")
    section_count = lax.axis_size("section")
    group_rank = lax.axis_index("group")
    seq_count, micro_count, row_count, model_width = inputs.shape
    seq_length = segments.shape[1]
    span_len = seq_length // micro_count
    tick_count = micro_count + section_count - 1
    slot_shape = (micro_count + 1, seq_count, row_count)
    forward_widths = [
        (model_width, jnp.bfloat16),
        (1, jnp.float32),
        (model_width, jnp.bfloat16),
        (model_width, jnp.bfloat16),
        (model_width, jnp.bfloat16),
        (model_width, jnp.float32),
        (1, jnp.float32),
        (model_width, jnp.bfloat16),
        (FF, jnp.float32),
        (FF, jnp.float32),
        (FF, jnp.bfloat16),
        (model_width, jnp.bfloat16),
    ]
    forward_stack = [
        jnp.zeros(slot_shape + (last_dim,), dtype_kind) for last_dim, dtype_kind in forward_widths
    ]
    key_cache = jnp.zeros((seq_count, seq_length, KV_HEADS, HEAD_DIM), jnp.bfloat16)
    value_cache = jnp.zeros_like(key_cache)
    received = jnp.zeros((seq_count, row_count, model_width), jnp.bfloat16)

    def front_part(x_span, cosine, sine_table):
        return project(weights, x_span, cosine, sine_table)

    def rear_part(x_span, query_rows, key_cache, value_cache, allowed):
        grouped, attention = attention_weights(query_rows, key_cache, allowed)
        context = jnp.einsum(
            "skgrt,stkd->srkgd",
            attention.astype(jnp.bfloat16),
            value_cache,
            preferred_element_type=jnp.float32,
        )
        context = context.reshape(x_span.shape[0], x_span.shape[1], D).astype(jnp.bfloat16)
        return (context,) + finish(weights, x_span, context)

    for tick_index in range(tick_count):
        span_index = tick_index - section_rank
        is_valid = (span_index >= 0) & (span_index < micro_count)
        span_at = jnp.clip(span_index, 0, micro_count - 1)
        slot_index = jnp.where(is_valid, span_index, micro_count)
        fresh_rows = lax.dynamic_index_in_dim(inputs, span_at, 1, keepdims=False)
        x_span = jnp.where(section_rank == 0, fresh_rows, received)
        cosine, sine_table, allowed = span_view(segments, span_at, group_rank, row_count, span_len)
        inverse, normed, query_rows, key_rows, value_rows = lax.cond(
            is_valid, front_part, project_zero, x_span, cosine, sine_table
        )
        key_span, value_span = (
            lax.all_gather(key_rows, "group", axis=1, tiled=True),
            lax.all_gather(value_rows, "group", axis=1, tiled=True),
        )
        key_cache = write_rows(key_cache, key_span, span_at * span_len, is_valid)
        value_cache = write_rows(value_cache, value_span, span_at * span_len, is_valid)
        context, output, hidden, inverse2, normed2, gate_value, upward, product = lax.cond(
            is_valid, rear_part, rear_zero, x_span, query_rows, key_cache, value_cache, allowed
        )
        values_now = [
            x_span,
            inverse,
            normed,
            query_rows.reshape(seq_count, row_count, model_width),
            context,
            hidden,
            inverse2,
            normed2,
            gate_value,
            upward,
            product,
            output,
        ]
        forward_stack = store(forward_stack, values_now, slot_index)
        received = passed_along(output, "section", 1)
    qkv_width = w_qkv.shape[2]
    backward_widths = [
        (qkv_width, jnp.bfloat16),
        (model_width, jnp.bfloat16),
        (FF, jnp.bfloat16),
        (FF, jnp.bfloat16),
        (model_width, jnp.bfloat16),
        (model_width, jnp.bfloat16),
    ]
    backward_stack = [
        jnp.zeros(slot_shape + (last_dim,), dtype_kind) for last_dim, dtype_kind in backward_widths
    ]
    key_grads = jnp.zeros((seq_count, seq_length, KV_HEADS, HEAD_DIM), jnp.float32)
    value_grads = jnp.zeros_like(key_grads)
    gain_first = jnp.zeros((model_width,), jnp.float32)
    gain_second = jnp.zeros((model_width,), jnp.float32)
    received_grad = jnp.zeros((seq_count, row_count, model_width), jnp.bfloat16)
    scale = HEAD_DIM ** (-0.5)

    def upper_part(
        grad_output,
        upward,
        gate_value,
        hidden,
        inverse2,
        query_flat,
        key_grads,
        value_grads,
        allowed,
    ):
        grad_product = jnp.einsum(
            "srd,fd->srf", grad_output, weights[5], preferred_element_type=jnp.float32
        )
        sigmoid_gate = jax.nn.sigmoid(gate_value)
        grad_gate = (
            grad_product * upward * sigmoid_gate * (1.0 + gate_value * (1.0 - sigmoid_gate))
        ).astype(jnp.bfloat16)
        grad_upward = (grad_product * gate_value * sigmoid_gate).astype(jnp.bfloat16)
        grad_normed2 = jnp.einsum(
            "srf,df->srd", grad_gate, weights[3], preferred_element_type=jnp.float32
        )
        grad_normed2 = grad_normed2 + jnp.einsum(
            "srf,df->srd", grad_upward, weights[4], preferred_element_type=jnp.float32
        )
        grad_hidden_norm, gain_two = rms_backward(hidden, inverse2, weights[7], grad_normed2)
        grad_hidden = grad_output.astype(jnp.float32) + grad_hidden_norm
        grad_hidden_low = grad_hidden.astype(jnp.bfloat16)
        grad_context = jnp.einsum(
            "sre,de->srd", grad_hidden_low, weights[2], preferred_element_type=jnp.float32
        ).astype(jnp.bfloat16)
        query_rows = query_flat.reshape(seq_count, row_count, HEADS, HEAD_DIM)
        grouped, attention = attention_weights(query_rows, key_cache, allowed)
        grad_grouped = grad_context.reshape(
            seq_count, row_count, KV_HEADS, HEADS // KV_HEADS, HEAD_DIM
        )
        grad_attention = jnp.einsum(
            "srkgd,stkd->skgrt", grad_grouped, value_cache, preferred_element_type=jnp.float32
        )
        grad_scores = (
            attention
            * (grad_attention - jnp.sum(attention * grad_attention, axis=-1, keepdims=True))
        ).astype(jnp.bfloat16)
        grad_query = (
            jnp.einsum(
                "skgrt,stkd->srkgd", grad_scores, key_cache, preferred_element_type=jnp.float32
            )
            * scale
        )
        key_grads = (
            key_grads
            + jnp.einsum(
                "skgrt,srkgd->stkd", grad_scores, grouped, preferred_element_type=jnp.float32
            )
            * scale
        )
        value_grads = value_grads + jnp.einsum(
            "skgrt,srkgd->stkd",
            attention.astype(jnp.bfloat16),
            grad_grouped,
            preferred_element_type=jnp.float32,
        )
        return (
            grad_gate,
            grad_upward,
            grad_hidden,
            grad_hidden_low,
            grad_query,
            gain_two,
            key_grads,
            value_grads,
        )

    def upper_zero(
        grad_output,
        upward,
        gate_value,
        hidden,
        inverse2,
        query_flat,
        key_grads,
        value_grads,
        allowed,
    ):
        lead = (seq_count, row_count)
        return (
            jnp.zeros(lead + (FF,), jnp.bfloat16),
            jnp.zeros(lead + (FF,), jnp.bfloat16),
            jnp.zeros(lead + (model_width,), jnp.float32),
            jnp.zeros(lead + (model_width,), jnp.bfloat16),
            jnp.zeros(lead + (KV_HEADS, HEADS // KV_HEADS, HEAD_DIM), jnp.float32),
            jnp.zeros((model_width,), jnp.float32),
            key_grads,
            value_grads,
        )

    def lower_part(
        grad_query, grad_keys, grad_values, cosine, sine_table, x_span, inverse, grad_hidden
    ):
        grad_query_lin = rotate_back(
            grad_query.reshape(seq_count, row_count, HEADS, HEAD_DIM), cosine, sine_table
        ).reshape(seq_count, row_count, model_width)
        grad_key_lin = rotate_back(grad_keys, cosine, sine_table).reshape(
            seq_count, row_count, KV_HEADS * HEAD_DIM
        )
        grad_value_lin = grad_values.reshape(seq_count, row_count, KV_HEADS * HEAD_DIM)
        grad_projected = jnp.concatenate(
            [grad_query_lin, grad_key_lin, grad_value_lin], axis=-1
        ).astype(jnp.bfloat16)
        grad_normed = jnp.einsum(
            "src,dc->srd", grad_projected, weights[0], preferred_element_type=jnp.float32
        )
        grad_input_norm, gain_one = rms_backward(
            x_span.astype(jnp.float32), inverse, weights[6], grad_normed
        )
        grad_input = (grad_hidden + grad_input_norm).astype(jnp.bfloat16)
        return (grad_projected, grad_input, gain_one)

    def lower_zero(
        grad_query, grad_keys, grad_values, cosine, sine_table, x_span, inverse, grad_hidden
    ):
        lead = (seq_count, row_count)
        return (
            jnp.zeros(lead + (qkv_width,), jnp.bfloat16),
            jnp.zeros(lead + (model_width,), jnp.bfloat16),
            jnp.zeros((model_width,), jnp.float32),
        )

    for tick_index in range(tick_count):
        span_index = micro_count - 1 - tick_index + (section_count - 1 - section_rank)
        is_valid = (span_index >= 0) & (span_index < micro_count)
        span_at = jnp.clip(span_index, 0, micro_count - 1)
        slot_index = jnp.where(is_valid, span_index, micro_count)
        given = lax.dynamic_index_in_dim(cotangent, span_at, 1, keepdims=False)
        grad_output = jnp.where(section_rank == section_count - 1, given, received_grad)
        grad_output = jnp.where(is_valid, grad_output, jnp.zeros_like(grad_output))
        kept_values = [
            lax.dynamic_index_in_dim(stack, span_at, 0, keepdims=False) for stack in forward_stack
        ]
        (
            x_span,
            inverse,
            normed,
            query_flat,
            context,
            hidden,
            inverse2,
            normed2,
            gate_value,
            upward,
            product,
            output,
        ) = kept_values
        cosine, sine_table, allowed = span_view(segments, span_at, group_rank, row_count, span_len)
        (
            grad_gate,
            grad_upward,
            grad_hidden,
            grad_hidden_low,
            grad_query,
            gain_two,
            key_grads,
            value_grads,
        ) = lax.cond(
            is_valid,
            upper_part,
            upper_zero,
            grad_output,
            upward,
            gate_value,
            hidden,
            inverse2,
            query_flat,
            key_grads,
            value_grads,
            allowed,
        )
        start_row = span_at * span_len
        key_piece = lax.dynamic_slice_in_dim(key_grads, start_row, span_len, 1)
        value_piece = lax.dynamic_slice_in_dim(value_grads, start_row, span_len, 1)
        grad_keys, grad_values = (
            lax.psum_scatter(
                key_piece.astype(jnp.bfloat16), "group", scatter_dimension=1, tiled=True
            ).astype(jnp.float32),
            lax.psum_scatter(
                value_piece.astype(jnp.bfloat16), "group", scatter_dimension=1, tiled=True
            ).astype(jnp.float32),
        )
        grad_projected, grad_input, gain_one = lax.cond(
            is_valid,
            lower_part,
            lower_zero,
            grad_query,
            grad_keys,
            grad_values,
            cosine,
            sine_table,
            x_span,
            inverse,
            grad_hidden,
        )
        gain_first = gain_first + jnp.where(is_valid, gain_one, jnp.zeros_like(gain_one))
        gain_second = gain_second + jnp.where(is_valid, gain_two, jnp.zeros_like(gain_two))
        backward_stack = store(
            backward_stack,
            [grad_projected, grad_hidden_low, grad_gate, grad_upward, grad_output, grad_input],
            slot_index,
        )
        received_grad = passed_along(grad_input, "section", -1)

    def flatten(stack):
        return stack[:micro_count].reshape(-1, stack.shape[-1])

    def cross(left_stack, right_stack):
        return lax.dot_general(
            flatten(left_stack),
            flatten(right_stack),
            (((0,), (0,)), ((), ())),
            preferred_element_type=jnp.float32,
        )

    normed_stack, context_stack, normed2_stack, product_stack = (
        forward_stack[2],
        forward_stack[4],
        forward_stack[7],
        forward_stack[10],
    )
    projected_grads, hidden_grads, gate_grads, upward_grads, output_grads, input_grads = (
        backward_stack
    )
    bias_grad = jnp.sum(flatten(projected_grads).astype(jnp.float32), axis=0)
    split_at = model_width + KV_HEADS * HEAD_DIM
    local_grads = (
        cross(normed_stack, projected_grads),
        bias_grad[:split_at],
        bias_grad[split_at:],
        cross(context_stack, hidden_grads),
        cross(normed2_stack, gate_grads),
        cross(normed2_stack, upward_grads),
        cross(product_stack, output_grads),
        gain_first,
        gain_second,
    )
    owned = (
        lax.psum_scatter(
            local_grads[0].astype(jnp.bfloat16), "group", scatter_dimension=0, tiled=True
        ).astype(jnp.float32),
        lax.psum_scatter(
            local_grads[1].astype(jnp.bfloat16), "group", scatter_dimension=0, tiled=True
        ).astype(jnp.float32),
        lax.psum_scatter(
            local_grads[2].astype(jnp.bfloat16), "group", scatter_dimension=0, tiled=True
        ).astype(jnp.float32),
        lax.psum_scatter(
            local_grads[3].astype(jnp.bfloat16), "group", scatter_dimension=0, tiled=True
        ).astype(jnp.float32),
        lax.psum_scatter(
            local_grads[4].astype(jnp.bfloat16), "group", scatter_dimension=0, tiled=True
        ).astype(jnp.float32),
        lax.psum_scatter(
            local_grads[5].astype(jnp.bfloat16), "group", scatter_dimension=0, tiled=True
        ).astype(jnp.float32),
        lax.psum_scatter(
            local_grads[6].astype(jnp.bfloat16), "group", scatter_dimension=0, tiled=True
        ).astype(jnp.float32),
        lax.psum_scatter(
            local_grads[7].astype(jnp.bfloat16), "group", scatter_dimension=0, tiled=True
        ).astype(jnp.float32),
        lax.psum_scatter(
            local_grads[8].astype(jnp.bfloat16), "group", scatter_dimension=0, tiled=True
        ).astype(jnp.float32),
    )
    summed = (
        lax.psum(owned[0].astype(jnp.bfloat16), "replica").astype(jnp.float32),
        lax.psum(owned[1].astype(jnp.bfloat16), "replica").astype(jnp.float32),
        lax.psum(owned[2].astype(jnp.bfloat16), "replica").astype(jnp.float32),
        lax.psum(owned[3].astype(jnp.bfloat16), "replica").astype(jnp.float32),
        lax.psum(owned[4].astype(jnp.bfloat16), "replica").astype(jnp.float32),
        lax.psum(owned[5].astype(jnp.bfloat16), "replica").astype(jnp.float32),
        lax.psum(owned[6].astype(jnp.bfloat16), "replica").astype(jnp.float32),
        lax.psum(owned[7].astype(jnp.bfloat16), "replica").astype(jnp.float32),
        lax.psum(owned[8].astype(jnp.bfloat16), "replica").astype(jnp.float32),
    )
    block_out = forward_stack[11][:micro_count].transpose(1, 0, 2, 3)[None]
    input_grad = input_grads[:micro_count].transpose(1, 0, 2, 3)[None]
    return (
        block_out,
        input_grad,
        summed[0][None],
        summed[1][None],
        summed[2][None],
        summed[3][None],
        summed[4][None],
        summed[5][None],
        summed[6][None],
        summed[7][None],
        summed[8][None],
    )


def solution(mesh):
    in_specs = (
        P("replica", None, "group", None),
        P("replica", None, "group", None),
        P("replica", None),
        P("section", "group", None),
        P("section", "group"),
        P("section", "group", None),
        P("section", "group", None),
        P("section", "group", None),
        P("section", "group", None),
        P("section", "group"),
        P("section", "group"),
    )
    out_specs = (
        P("section", "replica", None, "group", None),
        P("section", "replica", None, "group", None),
        P("section", "group", None),
        P("section", "group"),
        P("section", "group"),
        P("section", "group", None),
        P("section", "group", None),
        P("section", "group", None),
        P("section", "group", None),
        P("section", "group"),
        P("section", "group"),
    )
    return jax.shard_map(body, mesh=mesh, in_specs=in_specs, out_specs=out_specs, check_vma=False)
```

profile of v0, /device:TPU:1, one launch (start us, length us, event | category | flops | bytes accessed | tf_op | source)
XLA Modules:
  0.0 1808.2 jit_solution(1887665614126818370)
XLA Ops:
  15.9 37.2 %all-reduce.13 = (bf16[896]{0:T(1024)(128)(2,1)}, bf16[1152]{0:T(1024)(128)(2,1)}, bf16[896]{0:T(1024)(128)(2,1)}) all-reduce(bf16[896]{0:T(1024)(128)(2,1)S(1)} %dynamic-update-slice, bf16[1152]{0:T(1024)(128)(2,1)S(1)} %dynamic-update-slice.1, ...), channel_id=2, replica_groups=mesh['section'=2,'group'=16,'replica'=4] {'group'}, use_global_device_ids=true, to_apply=%add | all-reduce | flops 2944 | bytes 11776 | tf_op jit(solution)/shard_map/all_gather | solution.py:186
  58.8 6.3 conditional.12
  65.4 17.4 all_gather.45
  82.8 19.4 %all_gather.46 = bf16[1,1024,2,64]{3,2,0,1:T(2,128)(2,1)S(1)} all-gather(bf16[1,64,2,64]{3,2,0,1:T(2,128)(2,1)S(1)} %bitcast.1183), channel_id=1, replica_groups=mesh['section'=2,'group'=16,'replica'=4] {'group'}, dimensions={1}, use_global_device_ids=true | all-gather | bytes 278528 | tf_op jit(solution)/shard_map/all_gather | solution.py:245
  106.0 72.3 %all-gather.18.cloned.1.call-done = bf16[1,896,4864]{2,1,0:T(8,128)(2,1)} async-done(((bf16[1,56,4864]{2,1,0:T(8,128)(2,1)}), bf16[1,896,4864]{2,1,0:T(8,128)(2,1)}) %all-gather.18.cloned.1.call-update) | async-done | bytes 8716304 | tf_op jit(solution)/shard_map/all_gather | solution.py:183
  178.2 74.0 %all-gather.20.cloned.1.call-done = bf16[1,896,4864]{2,1,0:T(8,128)(2,1)} async-done(((bf16[1,56,4864]{2,1,0:T(8,128)(2,1)}), bf16[1,896,4864]{2,1,0:T(8,128)(2,1)}) %all-gather.20.cloned.1.call-update) | async-done | bytes 8716304 | tf_op jit(solution)/shard_map/all_gather | solution.py:184
  252.2 74.0 %all-gather.22.cloned.1.call-done = bf16[1,4864,896]{2,1,0:T(8,128)(2,1)} async-done(((bf16[1,304,896]{2,1,0:T(8,128)(2,1)}), bf16[1,4864,896]{2,1,0:T(8,128)(2,1)}) %all-gather.22.cloned.1.call-update) | async-done | bytes 8716304 | tf_op jit(solution)/shard_map/all_gather | solution.py:185
  326.2 37.6 %conditional.13 = (bf16[1,64,896]{2,1,0:T(8,128)(2,1)}, bf16[1,1,64,896]{3,2,1,0:T(8,128)(2,1)S(1)}, bf16[1,1,64,896]{3,2,1,0:T(8,128)(2,1)}, f32[1,1,64,896]{3,...) conditional(s32[]{:T(128)} %convert_element_type.641, ...), branch_computations={%region_3.4_spmd, %region_4.8_spmd} | conditional | flops 2270854400 | bytes 123250912 | solution.py:249
  333.7 3.5 copy.202
  337.2 5.0 fusion.15
  346.0 6.1 fusion.26
  352.1 6.5 multiply_convert_fusion
  358.7 3.4 fusion.20
  372.4 15.1 conditional.14
  387.5 18.2 %all_gather.53 = bf16[1,1024,2,64]{3,2,0,1:T(2,128)(2,1)S(1)} all-gather(bf16[1,64,2,64]{3,2,0,1:T(2,128)(2,1)} %bitcast.250), channel_id=1, replica_groups=mesh['section'=2,'group'=16,'replica'=4] {'group'}, dimensions={1}, use_global_device_ids=true | all-gather | bytes 278528 | tf_op jit(solution)/shard_map/all_gather | solution.py:245
  405.6 17.4 all_gather.52
  427.8 44.4 %conditional.15 = (bf16[1,64,896]{2,1,0:T(8,128)(2,1)}, bf16[1,1,64,896]{3,2,1,0:T(8,128)(2,1)S(1)}, bf16[1,1,64,896]{3,2,1,0:T(8,128)(2,1)}, f32[1,1,64,896]{3,...) conditional(s32[]{:T(128)} %convert_element_type.643, ...), branch_computations={%region_11.12_spmd, %region_12.16_spmd} | conditional | flops 2270854400 | bytes 116828360 | solution.py:249
  437.9 3.5 copy.208
  441.4 5.0 fusion.46
  453.4 6.1 fusion.57
  459.6 6.5 multiply_convert_fusion.2
  466.1 3.4 fusion.51
  486.8 17.1 all_gather.55
  503.9 17.6 all_gather.54
  526.4 5.3 conditional.17
  539.8 11.4 conditional.18
  563.3 184.4 %reduce-scatter.34.cloned.1.call-done = bf16[64,128]{1,0:T(8,128)(2,1)} async-done(((bf16[1024,128]{1,0:T(8,128)(2,1)}), bf16[64,128]{1,0:T(8,128)(2,1)}) %reduce-scatter.34.cloned.1.call-update) | async-done | bytes 16400
  749.1 73.5 %reduce-scatter.36.cloned.1.call-done = bf16[64,128]{1,0:T(8,128)(2,1)} async-done(((bf16[1024,128]{1,0:T(8,128)(2,1)}), bf16[64,128]{1,0:T(8,128)(2,1)}) %reduce-scatter.36.cloned.1.call-update) | async-done | bytes 16400
  826.6 19.3 %collective-permute-done.2 = bf16[1,64,896]{2,1,0:T(8,128)(2,1)S(1)} collective-permute-done((bf16[1,64,896]{2,1,0:T(8,128)(2,1)}, bf16[1,64,896]{2,1,0:T(8,128)(2,1)S(1)}, u32[]{:S(2)}, u32[]{:S(2)}) %collective-permute-start.2) | collective-permute-done | bytes 114720 | tf_op jit(solution)/shard_map/ppermute | solution.py:21
  847.5 51.1 %conditional.20 = (f32[1,64,896]{2,1,0:T(8,128)S(1)}, f32[1,64,2,7,64]{4,1,3,2,0:T(8,128)}, f32[896]{0:T(1024)S(1)}, f32[1,2048,2,64]{1,3,2,0:T(8,128)}, f32[1,2...) conditional(s32[]{:T(128)} %convert_element_type.643, ...), branch_computations={%region_37.38_spmd, %region_38.44_spmd} | conditional | flops 3002430976 | bytes 250307776 | solution.py:450
  847.6 8.0 fusion.184
  855.6 4.0 fusion.321
  859.6 4.1 fusion.196
  877.2 4.7 fusion.173
  881.9 3.6 copy.231
  885.5 5.7 fusion.157
  898.6 3.8 copy.232
  906.7 3.8 copy.233
  917.6 59.1 %reduce-scatter.38.cloned.1.call-done = bf16[64,128]{1,0:T(8,128)(2,1)} async-done(((bf16[1024,128]{1,0:T(8,128)(2,1)}), bf16[64,128]{1,0:T(8,128)(2,1)}) %reduce-scatter.38.cloned.1.call-update) | async-done | bytes 16400
  979.5 72.7 %reduce-scatter.40.cloned.1.call-done = bf16[64,128]{1,0:T(8,128)(2,1)} async-done(((bf16[1024,128]{1,0:T(8,128)(2,1)}), bf16[64,128]{1,0:T(8,128)(2,1)}) %reduce-scatter.40.cloned.1.call-update) | async-done | bytes 16400
  1053.7 16.2 conditional.21
  1072.7 4.4 collective-permute-done.3
  1078.7 50.3 %conditional.22 = (f32[1,64,896]{2,1,0:T(8,128)S(1)}, f32[1,64,2,7,64]{4,1,3,2,0:T(8,128)}, f32[896]{0:T(1024)S(1)}, f32[1,2048,2,64]{1,3,2,0:T(8,128)}, f32[1,2...) conditional(s32[]{:T(128)} %convert_element_type.641, ...), branch_computations={%region_50.51_spmd, %region_51.57_spmd} | conditional | flops 3002430976 | bytes 249848992 | solution.py:450
  1078.7 8.0 fusion.247
  1086.7 4.0 fusion.322
  1091.5 4.0 fusion.259
  1108.9 4.6 fusion.236
  1115.9 5.5 fusion.220
  1129.0 3.9 copy.239
  1138.0 3.8 copy.240
  1153.9 52.5 %reduce-scatter.42.cloned.1.call-done = bf16[64,128]{1,0:T(8,128)(2,1)} async-done(((bf16[1024,128]{1,0:T(8,128)(2,1)}), bf16[64,128]{1,0:T(8,128)(2,1)}) %reduce-scatter.42.cloned.1.call-update) | async-done | bytes 16400
  1207.2 74.1 %reduce-scatter.44.cloned.1.call-done = bf16[64,128]{1,0:T(8,128)(2,1)} async-done(((bf16[1024,128]{1,0:T(8,128)(2,1)}), bf16[64,128]{1,0:T(8,128)(2,1)}) %reduce-scatter.44.cloned.1.call-update) | async-done | bytes 16400
  1282.2 8.1 conditional.23
  1296.9 4.9 bitcast_convert_fusion
  1308.3 5.8 bitcast_convert_fusion.1
  1317.7 5.9 bitcast_convert_fusion.2
  1329.2 30.6 %reduce-scatter.48.cloned.1.call-done = bf16[56,896]{1,0:T(8,128)(2,1)} async-done(((bf16[896,896]{1,0:T(8,128)(2,1)}), bf16[56,896]{1,0:T(8,128)(2,1)}) %reduce-scatter.48.cloned.1.call-update) | async-done | bytes 100368
  1359.8 77.8 %reduce-scatter.46.cloned.1.call-done = bf16[56,1152]{1,0:T(8,128)(2,1)} async-done(((bf16[896,1152]{1,0:T(8,128)(2,1)}), bf16[56,1152]{1,0:T(8,128)(2,1)}) %reduce-scatter.46.cloned.1.call-update) | async-done | bytes 129040
  1437.7 99.8 %reduce-scatter.54.cloned.1.call-done = bf16[304,896]{1,0:T(8,128)(2,1)} async-done(((bf16[4864,896]{1,0:T(8,128)(2,1)}), bf16[304,896]{1,0:T(8,128)(2,1)}) %reduce-scatter.54.cloned.1.call-update) | async-done | bytes 544784
  1537.5 98.7 %reduce-scatter.52.cloned.1.call-done = bf16[56,4864]{1,0:T(8,128)(2,1)} async-done(((bf16[896,4864]{1,0:T(8,128)(2,1)}), bf16[56,4864]{1,0:T(8,128)(2,1)}) %reduce-scatter.52.cloned.1.call-update) | async-done | bytes 544784
  1636.2 98.3 %reduce-scatter.50.cloned.1.call-done = bf16[56,4864]{1,0:T(8,128)(2,1)} async-done(((bf16[896,4864]{1,0:T(8,128)(2,1)}), bf16[56,4864]{1,0:T(8,128)(2,1)}) %reduce-scatter.50.cloned.1.call-update) | async-done | bytes 544784
  1737.2 31.6 %all-reduce.12 = (bf16[1024]{0:T(1024)(128)(2,1)S(1)}, bf16[128]{0:T(256)(128)(2,1)S(1)}, bf16[896]{0:T(1024)(128)(2,1)S(1)}, bf16[896]{0:T(1024)(128)(2,1)S(1)}) all-reduce(bf16[1024]{0:T(1024)(128)(2,1)S(1)} %slice.213, bf16[128]{0:T(256)(128)(2,1)S(1)} %slice.214, ...), channel_id=17, replica_groups=mesh['section'=2,'group'=16,'replica'=4] {'group'}, use_global_device_ids=true, to_apply=%region_66.67.clone | all-reduce | flops 2944 | bytes 11776
  1769.1 13.4 all-reduce.14
  1786.2 5.8 all-reduce.18.cloned.1.call-done
  (486 shorter events, 294.1 us)
Async XLA Ops:
  7.2 51.6 %all-gather.14.cloned.1.call-start = ((), (), s32[]{:S(2)}) async-start(), calls=%async_computation.11 | async-start | bytes 2193408 | tf_op jit(solution)/shard_map/all_gather | solution.py:180
  7.9 98.1 %all-gather.16.cloned.1.call-start = ((), (), s32[]{:S(2)}) async-start(), calls=%async_computation.12 | async-start | bytes 1705984 | tf_op jit(solution)/shard_map/all_gather | solution.py:182
  8.7 169.6 %all-gather.18.cloned.1.call-start = ((), (), s32[]{:S(2)}) async-start(), calls=%async_computation.13 | async-start | bytes 9261056 | tf_op jit(solution)/shard_map/all_gather | solution.py:183
  9.4 242.8 %all-gather.20.cloned.1.call-start = ((), (), s32[]{:S(2)}) async-start(), calls=%async_computation.14 | async-start | bytes 9261056 | tf_op jit(solution)/shard_map/all_gather | solution.py:184
  10.0 316.2 %all-gather.22.cloned.1.call-start = ((), (), s32[]{:S(2)}) async-start(), calls=%async_computation.15 | async-start | bytes 9261056 | tf_op jit(solution)/shard_map/all_gather | solution.py:185
  10.6 737.1 %reduce-scatter.34.cloned.1.call-start = ((), (), s32[]{:S(2)}) async-start(), calls=%async_computation.16 | async-start | bytes 278528
  54.9 51.0 %copy-start.31 = (bf16[3,1,64,896]{3,2,0,1:T(8,128)(2,1)}, bf16[3,1,64,896]{3,2,0,1:T(8,128)(2,1)S(1)}, u32[]{:S(2)}) copy-start(bf16[3,1,64,896]{3,2,0,1:T(8,128)(2,1)S(1)} %get-tuple-element.1562) | copy-start | bytes 1032196
  57.6 314.7 %copy-start.48 = (f32[64,32]{1,0:T(8,128)}, f32[64,32]{1,0:T(8,128)S(1)}, u32[]{:S(2)}) copy-start(f32[64,32]{1,0:T(8,128)S(1)} %get-tuple-element.1578) | copy-start | bytes 24580
  57.6 314.7 %copy-start.50 = (f32[64,32]{1,0:T(8,128)}, f32[64,32]{1,0:T(8,128)S(1)}, u32[]{:S(2)}) copy-start(f32[64,32]{1,0:T(8,128)S(1)} %get-tuple-element.1579) | copy-start | bytes 24580
  58.8 267.4 %copy-start.21 = (pred[1,1,1,64,2048]{4,3,2,1,0:T(8,128)(4,1)}, pred[1,1,1,64,2048]{4,3,2,1,0:T(8,128)(4,1)S(1)}, u32[]{:S(2)}) copy-start(pred[1,1,1,64,2048]{4,3,2,1,0:T(8,128)(4,1)S(1)} %get-tuple-element.1566) | copy-start | bytes 393220
  65.2 17.6 copy-start.64
  65.2 17.6 copy-start.80
  102.3 223.9 %copy-start.41 = (bf16[3,1,64,896]{3,2,0,1:T(8,128)(2,1)}, bf16[3,1,64,896]{3,2,0,1:T(8,128)(2,1)S(1)}, u32[]{:S(2)}) copy-start(bf16[3,1,64,896]{3,2,0,1:T(8,128)(2,1)S(1)} %bitcast_dynamic-update-slice_fusion.33) | copy-start | bytes 1032196
  337.2 7.1 copy-start.73
  346.0 12.7 slice-start
  346.0 12.7 slice-start.1
  352.1 6.5 slice-start.2
  363.9 7.8 copy-start.61
  363.9 7.8 copy-start.59
  363.9 8.4 copy-start.6
  363.9 7.7 collective-permute-start
  387.5 18.2 %copy-start.66 = (bf16[1,1,64,896]{3,2,1,0:T(8,128)(2,1)}, bf16[1,1,64,896]{3,2,1,0:T(8,128)(2,1)S(1)}, u32[]{:S(2)}) copy-start(bf16[1,1,64,896]{3,2,1,0:T(8,128)(2,1)S(1)} %get-tuple-element.1054) | copy-start | bytes 344068
  427.8 54.8 %copy-start.77 = (f32[3,1,64,1]{2,3,1,0:T(1,128)S(1)}, f32[3,1,64,1]{2,3,1,0:T(1,128)}, u32[]{:S(2)}) copy-start(f32[3,1,64,1]{2,3,1,0:T(1,128)} %copy-done.76) | copy-start | bytes 2308
  427.8 56.4 %copy-start.53 = (f32[64,32]{1,0:T(8,128)S(1)}, f32[64,32]{1,0:T(8,128)}, u32[]{:S(2)}) copy-start(f32[64,32]{1,0:T(8,128)} %get-tuple-element.1570) | copy-start | bytes 24580
  441.4 10.3 copy-start.74
  453.4 12.7 slice-start.3
  453.4 12.7 slice-start.4
  472.2 10.4 copy-start.62
  472.2 10.4 collective-permute-start.1
  477.0 49.4 %copy-start.72 = (bf16[896]{0:T(1024)(128)(2,1)S(1)}, bf16[896]{0:T(1024)(128)(2,1)}, u32[]{:S(2)}) copy-start(bf16[896]{0:T(1024)(128)(2,1)} %get-tuple-element.1446) | copy-start | bytes 5380
  486.8 17.2 copy-start.67
  531.7 8.1 copy-start.63
  539.7 307.8 %copy-start.78 = (f32[3,1,64,1]{2,3,1,0:T(1,128)}, f32[3,1,64,1]{2,3,1,0:T(1,128)S(1)}, u32[]{:S(2)}) copy-start(f32[3,1,64,1]{2,3,1,0:T(1,128)S(1)} %constant_dynamic-update-slice_fusion.9) | copy-start | bytes 2308
  539.8 20.6 %copy-start.81 = (f32[1,1,64,1]{2,3,1,0:T(1,128)S(1)}, f32[1,1,64,1]{2,3,1,0:T(1,128)}, u32[]{:S(2)}) copy-start(f32[1,1,64,1]{2,3,1,0:T(1,128)} %copy-done.80) | copy-start | bytes 772
  539.8 284.2 %copy-start.54 = (f32[64,32]{1,0:T(8,128)S(1)}, f32[64,32]{1,0:T(8,128)}, u32[]{:S(2)}) copy-start(f32[64,32]{1,0:T(8,128)} %get-tuple-element.1571) | copy-start | bytes 24580
  555.5 267.1 %reduce-scatter.36.cloned.1.call-start = ((), (), s32[]{:S(2)}) async-start(), calls=%async_computation.17 | async-start | bytes 278528
  559.8 416.9 %reduce-scatter.38.cloned.1.call-start = ((), (), s32[]{:S(2)}) async-start(), calls=%async_computation.18 | async-start | bytes 278528
  825.3 22.2 %copy-start.56 = (bf16[1,1,64,1152]{3,2,1,0:T(8,128)(2,1)}, bf16[1,1,64,1152]{3,2,1,0:T(8,128)(2,1)S(1)}, u32[]{:S(2)}) copy-start(bf16[1,1,64,1152]{3,2,1,0:T(8,128)(2,1)S(1)} %get-tuple-element.1056) | copy-start | bytes 442372
  825.3 20.6 %collective-permute-start.2 = (bf16[1,64,896]{2,1,0:T(8,128)(2,1)}, bf16[1,64,896]{2,1,0:T(8,128)(2,1)S(1)}, u32[]{:S(2)}, u32[]{:S(2)}) collective-permute-start(bf16[1,64,896]{2,1,0:T(8,128)(2,1)} %get-tuple-element.1041), channel_id=1, source_target_pairs={{64,0},{65,1},{66,2},{67,3},{68,4},{69,5},{70,6},{71,7},{72,8},{73... | collective-permute-start | bytes 344072 | tf_op jit(solution)/shard_map/ppermute | solution.py:21
  847.5 8.1 copy-start.1
  864.5 12.7 copy-start.33
  875.3 6.6 copy-start.9
  877.2 8.2 copy-start.70
  898.6 155.0 %copy-start.49 = (f32[64,32]{1,0:T(8,128)S(1)}, f32[64,32]{1,0:T(8,128)}, u32[]{:S(2)}) copy-start(f32[64,32]{1,0:T(8,128)} %copy-done.48) | copy-start | bytes 24580
  898.6 155.0 %copy-start.51 = (f32[64,32]{1,0:T(8,128)S(1)}, f32[64,32]{1,0:T(8,128)}, u32[]{:S(2)}) copy-start(f32[64,32]{1,0:T(8,128)} %copy-done.50) | copy-start | bytes 24580
  904.6 174.1 %copy-start.22 = (pred[1,1,1,64,2048]{4,3,2,1,0:T(8,128)(4,1)S(1)}, pred[1,1,1,64,2048]{4,3,2,1,0:T(8,128)(4,1)}, u32[]{:S(2)}) copy-start(pred[1,1,1,64,2048]{4,3,2,1,0:T(8,128)(4,1)} %copy-done.21) | copy-start | bytes 393220
  906.7 145.6 %reduce-scatter.40.cloned.1.call-start = ((), (), s32[]{:S(2)}) async-start(), calls=%async_computation.19 | async-start | bytes 278528
  914.8 291.7 %reduce-scatter.42.cloned.1.call-start = ((), (), s32[]{:S(2)}) async-start(), calls=%async_computation.20 | async-start | bytes 278528
  1069.9 8.8 copy-start.58
  1069.9 7.3 collective-permute-start.3
  1078.7 8.0 copy-start.2
  1096.3 12.6 copy-start.36
  1107.0 6.6 copy-start.11
  1129.0 21.3 %copy-start.65 = (bf16[1,1,64,896]{3,2,1,0:T(8,128)(2,1)S(1)}, bf16[1,1,64,896]{3,2,1,0:T(8,128)(2,1)}, u32[]{:S(2)}) copy-start(bf16[1,1,64,896]{3,2,1,0:T(8,128)(2,1)} %copy-done.64) | copy-start | bytes 344068
  1129.0 23.9 %copy-start.57 = (bf16[1,1,64,1152]{3,2,1,0:T(8,128)(2,1)S(1)}, bf16[1,1,64,1152]{3,2,1,0:T(8,128)(2,1)}, u32[]{:S(2)}) copy-start(bf16[1,1,64,1152]{3,2,1,0:T(8,128)(2,1)} %copy-done.56) | copy-start | bytes 442372
  1129.0 153.2 %copy-start.32 = (bf16[3,1,64,896]{3,2,0,1:T(8,128)(2,1)S(1)}, bf16[3,1,64,896]{3,2,0,1:T(8,128)(2,1)}, u32[]{:S(2)}) copy-start(bf16[3,1,64,896]{3,2,0,1:T(8,128)(2,1)} %get-tuple-element.1480) | copy-start | bytes 1032196
  1135.3 146.1 %reduce-scatter.44.cloned.1.call-start = ((), (), s32[]{:S(2)}) async-start(), calls=%async_computation.21 | async-start | bytes 278528
  1144.2 215.7 %reduce-scatter.48.cloned.1.call-start = ((), (), s32[]{:S(2)}) async-start(), calls=%async_computation.23 | async-start | bytes 1705984
  1150.2 287.5 %reduce-scatter.46.cloned.1.call-start = ((), (), s32[]{:S(2)}) async-start(), calls=%async_computation.22 | async-start | bytes 2193408
  1290.3 6.6 copy-start.45
  1293.4 244.1 %reduce-scatter.54.cloned.1.call-start = ((), (), s32[]{:S(2)}) async-start(), calls=%async_computation.26 | async-start | bytes 9261056
  1301.9 334.3 %reduce-scatter.52.cloned.1.call-start = ((), (), s32[]{:S(2)}) async-start(), calls=%async_computation.25 | async-start | bytes 9261056
  1314.1 420.4 %reduce-scatter.50.cloned.1.call-start = ((), (), s32[]{:S(2)}) async-start(), calls=%async_computation.24 | async-start | bytes 9261056
  1323.6 468.4 %all-reduce.18.cloned.1.call-start = ((), (), s32[]{:S(2)}) async-start(), calls=%async_computation.27 | async-start | bytes 3727360 | tf_op jit(solution)/shard_map/psum | solution.py:560
  (32 other events, 113.6 us)
Sparse Core Ops, SparseCore 0:
  10.2 47.5 all-gather.13
  59.9 43.5 all-gather.15
  105.7 72.5 all-gather.17
  180.2 71.9 all-gather.19
  254.2 71.9 all-gather.21
  555.6 192.0 reduce-scatter.33
  751.2 71.3 reduce-scatter.35
  906.8 69.8 reduce-scatter.37
  980.8 71.4 reduce-scatter.39
  1135.4 71.0 reduce-scatter.41
  1209.9 71.3 reduce-scatter.43
  1284.6 75.1 reduce-scatter.47
  1363.5 74.0 reduce-scatter.45
  1441.4 96.0 reduce-scatter.53
  1541.2 94.9 reduce-scatter.51
  1639.9 94.5 reduce-scatter.49
  1737.5 54.4 all-reduce.17
where the time goes:
time: 1820 us; the launch traced here: 1810 us
  waiting for transfers between devices  1170 us (64%)
  local copies, waits for them, and re-layouts  194 us (11%)
  blocking collectives  189 us (10%)
  matrix products  149 us (8%)
  other arithmetic  73.8 us (4%)
  between operations  18.3 us (1%)
    unnamed x28, waiting for transfers between devices  925 us
    all_gather x1, waiting for transfers between devices, body(): lax.all_gather(shards[4], 'group', axis=0, tiled=True)  74 us
    all_gather x1, waiting for transfers between devices, body(): lax.all_gather(shards[5], 'group', axis=0, tiled=True)  74 us
    all_gather x1, waiting for transfers between devices, body(): lax.all_gather(shards[3], 'group', axis=0, tiled=True)  72.3 us
    dynamic_update_slice x48, local copies, waits for them, and re-layouts, store(): lax.dynamic_update_index_in_dim(stack, value, slot_index, 0)  54.9 us
    all_gather x3, blocking collectives, body(): lax.all_gather(value_rows, 'group', axis=1, tiled=True)  54.7 us
    all_gather x3, blocking collectives, body(): lax.all_gather(key_rows, 'group', axis=1, tiled=True)  52.4 us
    another operation x48, local copies, waits for them, and re-layouts  43.4 us
  transfers between devices with their start and end apart: 21, of which 17 were waited for; matrix products, arithmetic and copies ran while one was open for 7% of the time, Pallas kernels for 0%

commit v1 on v0

v1 whole, which is shorter than its diff:
```python
import functools

import jax
import jax.numpy as jnp
import numpy as np
from jax import lax
from jax.experimental import pallas as pl
from jax.experimental.pallas import tpu as pltpu
from jax.sharding import PartitionSpec as P

D = 896
HEADS = 14
KV = 128
HALF = 32
FF = 4864
QUARTER = FF // 4
QKV = 1152
ROWS = 128
SPAN = 1024
LEN = 2048
PAIRS = 7
EPSILON = 1e-06
THETA = 1000000.0
NEGATIVE = -1e30
SCALE = 0.125
VMEM_LIMIT = 56 * 1024 * 1024
MESH = pl.DeviceIdType.MESH
BF = jnp.bfloat16
F32 = jnp.float32
VMEM_SPEC = pl.BlockSpec(memory_space=pltpu.VMEM)
ANY_SPEC = pl.BlockSpec(memory_space=pl.ANY)


def nn(a, b):
    return lax.dot_general(a, b, (((1,), (0,)), ((), ())), preferred_element_type=F32)


def nt(a, b):
    return lax.dot_general(a, b, (((1,), (1,)), ((), ())), preferred_element_type=F32)


def tn(a, b):
    return lax.dot_general(a, b, (((0,), (0,)), ((), ())), preferred_element_type=F32)


def params(collective_id=None):
    if collective_id is None:
        return pltpu.CompilerParams(vmem_limit_bytes=VMEM_LIMIT)
    return pltpu.CompilerParams(
        vmem_limit_bytes=VMEM_LIMIT, collective_id=collective_id, has_side_effects=True
    )


def shaped(*shape, dtype=BF):
    return jax.ShapeDtypeStruct(shape, dtype)


def local_call(kernel, name, out_shape, scratch=()):
    return pl.pallas_call(
        kernel,
        out_shape=out_shape,
        scratch_shapes=list(scratch),
        compiler_params=params(),
        name=name,
    )


def signal(devices):
    barrier = pltpu.get_barrier_semaphore()
    for device in devices:
        pl.semaphore_signal(barrier, inc=1, device_id=device, device_id_type=MESH)


def greeted(count):
    pl.semaphore_wait(pltpu.get_barrier_semaphore(), count)


def grid_place():
    me = lax.axis_index("group")
    z = me // 4
    y = lax.rem(me, 4)

    def along_y(step):
        return {"group": z * 4 + lax.rem(y + step, 4)}

    def along_z(step):
        return {"group": lax.rem(z + step, 4) * 4 + y}

    return z, y, along_y, along_z


def neighbours(along_y, along_z):
    return [along_y(1), along_y(3), along_z(1), along_z(3)]


class Copies:
    def __init__(self, send, recv):
        self.send, self.recv, self.used = send, recv, 0

    def __call__(self, src, dst, device):
        index = self.used
        self.used += 1
        each = pltpu.make_async_remote_copy(
            src_ref=src,
            dst_ref=dst,
            send_sem=self.send.at[index],
            recv_sem=self.recv.at[index],
            device_id=device,
            device_id_type=MESH,
        )
        each.start()
        return each


def gather_phase(firsts, seconds, place, device_at, copies):
    def copy(block, slot, step):
        return copies(block(slot), block(slot), device_at(step))

    firsts_right = [copy(block, place, 1) for block in firsts]
    seconds_left = [copy(block, place, 3) for block in seconds]
    others = [copy(block, place, 3) for block in firsts] + [copy(block, place, 1) for block in seconds]

    def relay():
        relays = []
        for block, came in zip(firsts, firsts_right):
            came.wait_recv()
            relays.append(copy(block, lax.rem(place + 3, 4), 1))
        for block, came in zip(seconds, seconds_left):
            came.wait_recv()
            relays.append(copy(block, lax.rem(place + 1, 4), 3))

        def finish():
            for each in others + relays:
                each.wait_recv()
            for each in firsts_right + seconds_left + others + relays:
                each.wait_send()

        return finish

    return relay


def gather_both(first_a, second_a, first_b, second_b, copies):
    z, y, along_y, along_z = grid_place()
    relay_a = gather_phase([first_a[0]], [second_a[0]], y, along_y, copies)
    relay_b = gather_phase([first_b[0]], [second_b[0]], z, along_z, copies)
    yield
    finish_a = relay_a()
    finish_b = relay_b()
    yield
    finish_a()
    relay_a = gather_phase([first_a[1]], [second_a[1]], z, along_z, copies)
    finish_b()
    relay_b = gather_phase([first_b[1]], [second_b[1]], y, along_y, copies)
    yield
    finish_a = relay_a()
    finish_b = relay_b()
    yield
    finish_a()
    finish_b()


def run(steps):
    for _ in steps:
        pass


def y_then_z(ref, *tail):
    z = lax.axis_index("group") // 4
    return (lambda at: ref.at[(z, at, *tail)]), (lambda at: ref.at[(at, slice(None), *tail)])


def z_then_y(ref, *tail):
    y = lax.rem(lax.axis_index("group"), 4)
    return (lambda at: ref.at[(at, y, *tail)]), (lambda at: ref.at[(slice(None), at, *tail)])


def quarter_route():
    group, replica = lax.axis_index("group"), lax.axis_index("replica")
    target = {"group": 4 * lax.rem(group, 4) + replica, "replica": group // 4}
    source = {"group": 4 * replica + group // 4, "replica": lax.rem(group, 4)}
    stays = (target["group"] == group) & (target["replica"] == replica)
    return target, source, stays


def first_kernel(
    gate, up, down, qkv, out, x_ref, cos_ref, sin_ref, kseg_ref,
    gate_all, up_all, down_all, qkv_w, out_w, bias_ref, gain1_ref, gain2_ref, hidden_ref, normed2_ref,
    qkv_all, out_all, normed_ref, q_ref, kv_ref, context_ref, keys_ref, values_ref, bias0, bias1, send, recv, local
):
    z, y, along_y, along_z = grid_place()
    core = lax.rem(lax.axis_index("replica"), 2)
    mate = {"replica": lax.axis_index("replica") + 1 - 2 * core}
    target, source, stays = quarter_route()
    moves = jnp.logical_not(stays)
    signal(neighbours(along_y, along_z) + [mate])
    places = (qkv_all.at[core, z, y], out_all.at[core, z, y], gate_all.at[z, y], up_all.at[z, y])
    own = []
    for index, (src, dst) in enumerate(zip((qkv, out, gate, up), places)):
        own.append(pltpu.make_async_copy(src, dst, local.at[index]))
        own[-1].start()
    there = target["group"]
    moved = pltpu.make_async_remote_copy(
        src_ref=down,
        dst_ref=down_all.at[there // 4, lax.rem(there, 4)],
        send_sem=local.at[5],
        recv_sem=local.at[6],
        device_id=target,
        device_id_type=MESH,
    )
    stayed = pltpu.make_async_copy(down, down_all.at[z, y], local.at[4])

    @pl.when(moves)
    def _():
        signal([source])
        greeted(6)
        moved.start()

    @pl.when(stays)
    def _():
        greeted(5)
        stayed.start()

    copies = Copies(send, recv)
    own[0].wait()
    own[1].wait()
    top, bottom = (slice(0, 16), slice(None)), (slice(16, 32), slice(None))
    dense = gather_both(
        y_then_z(qkv_all.at[core], *top),
        y_then_z(qkv_all.at[core], *bottom),
        z_then_y(out_all.at[core], *top),
        z_then_y(out_all.at[core], *bottom),
        copies,
    )
    next(dense)
    next(dense)
    next(dense)
    own[2].wait()
    own[3].wait()

    @pl.when(moves)
    def _():
        moved.wait()

    @pl.when(stays)
    def _():
        stayed.wait()

    left, right = (slice(None), slice(0, 512)), (slice(None), slice(512, D))
    wide = gather_both(
        y_then_z(gate_all), y_then_z(down_all, *left), z_then_y(up_all), z_then_y(down_all, *right), copies
    )
    next(wide)
    next(dense)
    next(wide)
    run(dense)
    halves = [copies(ref.at[core], ref.at[core], mate) for ref in (qkv_all, out_all)]
    next(wide)
    for each in halves:
        each.wait()
    for at in range(16):
        rows, cut = 56 * at, 56 * at + 32
        qkv_w[rows:cut] = qkv_all[0, at // 4, at % 4]
        qkv_w[cut : rows + 56] = qkv_all[1, at // 4, at % 4, :24]
        out_w[rows:cut] = out_all[0, at // 4, at % 4]
        out_w[cut : rows + 56] = out_all[1, at // 4, at % 4, :24]
    small = [qkv_all[1, at // 4, at % 4, 24:32].astype(F32)[:1] for at in range(16)]
    bias_ref[...] = jnp.concatenate([each[:, :72] for each in small], axis=1)
    gain1_ref[...] = jnp.concatenate([each[:, 72:128] for each in small], axis=1)
    gain2_ref[...] = jnp.concatenate([each[:, 128:184] for each in small], axis=1)
    front_work(x_ref, qkv_w, bias_ref, gain1_ref, cos_ref, sin_ref, normed_ref, q_ref, kv_ref, copies, lambda: None)
    next(wide)
    attention_work(
        x_ref, q_ref, kv_ref, kseg_ref, out_w, gain2_ref, context_ref, hidden_ref, normed2_ref,
        keys_ref, values_ref, bias0, bias1
    )
    run(wide)


def first(gate, up, down, qkv, out, x, cosine, sine, kseg):
    return pl.pallas_call(
        first_kernel,
        out_shape=(
            shaped(4, 4, *gate.shape),
            shaped(4, 4, *up.shape),
            shaped(4, 4, *down.shape),
            shaped(D, QKV),
            shaped(D, D),
            shaped(1, QKV, dtype=F32),
            shaped(1, D, dtype=F32),
            shaped(1, D, dtype=F32),
            shaped(ROWS, D, dtype=F32),
            shaped(ROWS, D),
        ),
        in_specs=[ANY_SPEC] * 5 + [VMEM_SPEC] * 4,
        out_specs=[ANY_SPEC] * 3 + [VMEM_SPEC] * 7,
        scratch_shapes=[
            pltpu.VMEM((2, 4, 4, *qkv.shape), BF),
            pltpu.VMEM((2, 4, 4, *out.shape), BF),
            pltpu.VMEM((ROWS, D), BF),
            pltpu.VMEM((ROWS, D), BF),
            pltpu.VMEM((2, 4, 4, 64, 2 * KV), BF),
            pltpu.VMEM((ROWS, D), BF),
        ]
        + ATTENTION_SCRATCH
        + [
            pltpu.SemaphoreType.DMA((74,)),
            pltpu.SemaphoreType.DMA((74,)),
            pltpu.SemaphoreType.DMA((7,)),
        ],
        compiler_params=params(0),
        name="first",
    )(gate, up, down, qkv, out, x, cosine, sine, kseg)


def scatter_phase(firsts, seconds, place, device_at, copies):
    right, left, far = (lax.rem(place + step, 4) for step in (1, 3, 2))

    def load(ref):
        return ref[...].astype(F32)

    first_far = [copies(block(far), bufs[0], device_at(1)) for block, bufs, put in firsts]
    second_far = [copies(block(far), bufs[0], device_at(3)) for block, bufs, put in seconds]
    first_near = [copies(block(left), bufs[2], device_at(3)) for block, bufs, put in firsts]
    second_near = [copies(block(right), bufs[1], device_at(1)) for block, bufs, put in seconds]

    def pass_on():
        first_sum, second_sum = [], []
        for came, (block, bufs, put) in zip(first_far, firsts):
            came.wait_recv()
            bufs[3][...] = (load(block(right)) + load(bufs[0])).astype(BF)
            first_sum.append(copies(bufs[3], bufs[1], device_at(1)))
        for came, (block, bufs, put) in zip(second_far, seconds):
            came.wait_recv()
            bufs[3][...] = (load(block(left)) + load(bufs[0])).astype(BF)
            second_sum.append(copies(bufs[3], bufs[2], device_at(3)))

        def finish():
            near, far_sum = first_near + second_near, first_sum + second_sum
            for one, two, (block, bufs, put) in zip(near, far_sum, firsts + seconds):
                one.wait_recv()
                two.wait_recv()
                put(load(block(place)) + load(bufs[1]) + load(bufs[2]))
            for each in first_far + second_far + near + far_sum:
                each.wait_send()

        return finish

    return pass_on


def scatter_both(first_a, second_a, first_b, second_b, copies):
    z, y, along_y, along_z = grid_place()

    def wide(parts):
        out = []
        for block, bufs, kept, _, _ in parts:
            def put(value, kept=kept):
                kept[...] = value.astype(BF)

            out.append((block, bufs, put))
        return out

    def slim(parts):
        return [((lambda at, kept=kept: kept.at[at]), bufs, put) for _, _, kept, bufs, put in parts]

    pass_a = scatter_phase(wide(first_a), wide(second_a), y, along_y, copies)
    pass_b = scatter_phase(wide(first_b), wide(second_b), z, along_z, copies)
    yield
    finish_a = pass_a()
    finish_b = pass_b()
    finish_a()
    pass_a = scatter_phase(slim(first_a), slim(second_a), z, along_z, copies)
    finish_b()
    pass_b = scatter_phase(slim(first_b), slim(second_b), y, along_y, copies)
    finish_a = pass_a()
    finish_b = pass_b()
    finish_a()
    finish_b()


def scatter_scratch(*shapes):
    scratch = []
    for shape in shapes:
        scratch += [pltpu.VMEM((4, *shape), BF)] * 5 + [pltpu.VMEM(shape, BF)] * 4
    return scratch


def scatter_part(scratch, index, block, put):
    mine = scratch[9 * index : 9 * index + 9]
    return block, mine[:4], mine[4], mine[5:], put


def stored_in(ref, *at):
    def put(value):
        ref[at if at else ...] = value.astype(ref.dtype)

    return put


DOWN_STARTS = (0, 80, 160, 224)
DOWN_ROWS = 80


def mlp_terms(rows_ref, dgate_ref, dup_ref, product_ref, dout_ref, gate_terms, up_terms, down_terms):
    def flat(ref):
        return ref[...].reshape(4 * ROWS, ref.shape[-1])

    rows = flat(rows_ref)
    for terms, grads in ((gate_terms, dgate_ref), (up_terms, dup_ref)):
        whole = tn(rows, flat(grads))
        for at in range(16):
            terms[at // 4, at % 4] = whole[56 * at : 56 * at + 56].astype(BF)
    whole = tn(flat(product_ref), flat(dout_ref)).astype(BF)
    for at in range(16):
        start = 304 * (at // 4) + DOWN_STARTS[at % 4]
        down_terms[at // 4, at % 4] = whole[start : start + DOWN_ROWS]


def mlp_sums(gate_terms, up_terms, down_terms, gate_out, up_out, down_out, scratch, copies):
    left, right = slice(0, 512), slice(512, D)
    return scatter_both(
        [scatter_part(scratch, 0, lambda at: gate_terms.at[:, at], stored_in(gate_out))],
        [
            scatter_part(
                scratch,
                2,
                lambda at: down_terms.at[:, at, :, left],
                stored_in(down_out, slice(None), left),
            )
        ],
        [scatter_part(scratch, 1, lambda at: up_terms.at[at], stored_in(up_out))],
        [
            scatter_part(
                scratch,
                3,
                lambda at: down_terms.at[at, :, :, right],
                stored_in(down_out, slice(None), right),
            )
        ],
        copies,
    )


MLP_SUMS_SHAPES = ((56, QUARTER), (56, QUARTER), (DOWN_ROWS, 512), (DOWN_ROWS, D - 512))


def qkv_scatter_kernel(
    normed_ref, dprojected_ref, small_ref, context_ref, dlow_ref, qkv_out, out_out, *rest
):
    qkv_terms, out_terms, qkv_landed, out_landed, qkv_half, out_half = rest[:6]
    scratch, (send, recv) = rest[6:-2], rest[-2:]
    z, y, along_y, along_z = grid_place()
    core = lax.rem(lax.axis_index("replica"), 2)
    mate = {"replica": lax.axis_index("replica") + 1 - 2 * core}
    signal(neighbours(along_y, along_z) + [mate])
    whole = tn(normed_ref[...], dprojected_ref[...])
    for at in range(16):
        rows = jnp.concatenate([whole[56 * at : 56 * at + 56], small_ref[at]], axis=0)
        qkv_terms[at // 4, at % 4] = rows.astype(BF)
    whole = tn(context_ref[...], dlow_ref[...])
    for at in range(16):
        rows = jnp.concatenate([whole[56 * at : 56 * at + 56], jnp.zeros((8, D), F32)], axis=0)
        out_terms[at // 4, at % 4] = rows.astype(BF)
    greeted(5)
    copies = Copies(send, recv)
    mine = pl.ds(pl.multiple_of(32 * core, 32), 32)
    theirs = pl.ds(pl.multiple_of(32 - 32 * core, 32), 32)
    pairs = ((qkv_terms, qkv_landed, qkv_half), (out_terms, out_landed, out_half))
    sent = [copies(terms.at[:, :, theirs], landed, mate) for terms, landed, half in pairs]
    for each, (terms, landed, half) in zip(sent, pairs):
        each.wait_recv()
        half[...] = (terms[:, :, mine].astype(F32) + landed[...].astype(F32)).astype(BF)
    top, bottom = pl.ds(0, 16), pl.ds(16, 16)
    steps = scatter_both(
        [scatter_part(scratch, 0, lambda at: qkv_half.at[:, at, top], stored_in(qkv_out, slice(0, 16)))],
        [scatter_part(scratch, 1, lambda at: qkv_half.at[:, at, bottom], stored_in(qkv_out, slice(16, 32)))],
        [scatter_part(scratch, 2, lambda at: out_half.at[at, :, top], stored_in(out_out, slice(0, 16)))],
        [scatter_part(scratch, 3, lambda at: out_half.at[at, :, bottom], stored_in(out_out, slice(16, 32)))],
        copies,
    )
    run(steps)
    for each in sent:
        each.wait_send()


def qkv_scatter(normed, dprojected, small, context, dlow):
    return pl.pallas_call(
        qkv_scatter_kernel,
        out_shape=(shaped(32, QKV, dtype=F32), shaped(32, D, dtype=F32)),
        scratch_shapes=[
            pltpu.VMEM((4, 4, 64, QKV), BF),
            pltpu.VMEM((4, 4, 64, D), BF),
            pltpu.VMEM((4, 4, 32, QKV), BF),
            pltpu.VMEM((4, 4, 32, D), BF),
            pltpu.VMEM((4, 4, 32, QKV), BF),
            pltpu.VMEM((4, 4, 32, D), BF),
        ]
        + scatter_scratch((16, QKV), (16, QKV), (16, D), (16, D))
        + [pltpu.SemaphoreType.DMA((32,)), pltpu.SemaphoreType.DMA((32,))],
        compiler_params=params(2),
        name="qkv_scatter",
    )(normed, dprojected, small, context, dlow)


def replica_partners():
    me = lax.axis_index("replica")
    return me, me + 1 - 2 * lax.rem(me, 2), lax.rem(me + 2, 4), 3 - me


def exchange(own_ref, all_ref, part, far_part, near_sum, part_in, far_in, near_in, copies, work):
    me, mate, next_, far = replica_partners()
    halves = (slice(0, 64), slice(64, 128))
    to_mate, to_next = {"replica": mate}, {"replica": next_}
    greeted(2)
    across = [copies(own_ref.at[half], all_ref.at[me, half], to_next) for half in halves]
    beside = copies(own_ref, all_ref.at[me], to_mate)
    all_ref[me] = own_ref[...]
    total = work([(me, slice(0, ROWS))])
    beside.wait_recv()
    part[...] = work([(mate, slice(0, ROWS))]).astype(BF)
    sent = [copies(part, part_in, to_mate)]
    forwards, sums = [], []
    for index, half in enumerate(halves):
        across[index].wait_recv()
        forwards.append(copies(all_ref.at[next_, half], all_ref.at[next_, half], to_mate))
        forwards[-1].wait_recv()
        terms = work([(next_, half), (far, half)])
        far_part[index] = terms[64:].astype(BF)
        passed = copies(far_part.at[index], far_in.at[index], to_mate)
        passed.wait_recv()
        near_sum[index] = (terms[:64] + far_in[index].astype(F32)).astype(BF)
        sums.append(copies(near_sum.at[index], near_in.at[index], to_next))
        sent.append(passed)
    sent[0].wait_recv()
    total = total + part_in[...].astype(F32)
    for each in sums:
        each.wait_recv()
    total = total + near_in[...].reshape(ROWS, D).astype(F32)
    for each in across + [beside] + forwards + sent + sums:
        each.wait_send()
    return total


EXCHANGE_SCRATCH = [
    pltpu.VMEM((D, QUARTER), BF),
    pltpu.VMEM((D, QUARTER), BF),
    pltpu.VMEM((QUARTER, D), BF),
    pltpu.VMEM((ROWS, D), BF),
    pltpu.VMEM((2, 64, D), BF),
    pltpu.VMEM((2, 64, D), BF),
    pltpu.VMEM((ROWS, D), BF),
    pltpu.VMEM((2, 64, D), BF),
    pltpu.VMEM((2, 64, D), BF),
    pltpu.SemaphoreType.DMA((10,)),
    pltpu.SemaphoreType.DMA((10,)),
    pltpu.SemaphoreType.DMA((18,)),
]


def mlp_start(hbm, vmem, local):
    me, mate, next_, far = replica_partners()
    signal([{"replica": mate}, {"replica": next_}])
    loads = [pltpu.make_async_copy(src, dst, local.at[i]) for i, (src, dst) in enumerate(zip(hbm[:2], vmem[:2]))]
    for at in range(16):
        skip = 80 * (at % 4) - DOWN_STARTS[at % 4]
        rows = pl.ds(304 * (at // 4) + 80 * (at % 4), DOWN_ROWS - skip)
        piece = hbm[2].at[at // 4, at % 4, pl.ds(skip, DOWN_ROWS - skip)]
        loads.append(pltpu.make_async_copy(piece, vmem[2].at[rows], local.at[2 + at]))
    for each in loads:
        each.start()
    return loads


def split_rows(value, parts):
    start = 0
    for source, rows in parts:
        count = rows.stop - rows.start
        yield source, rows, value[start : start + count]
        start += count


def mlp_forward_kernel(
    normed_ref, hidden_ref, gate_hbm, up_hbm, down_hbm, out_ref, all_ref, gate_ref, up_ref,
    gate_w, up_w, down_w, part, far_part, near_sum, part_in, far_in, near_in, send, recv, local
):
    loads = mlp_start((gate_hbm, up_hbm, down_hbm), (gate_w, up_w, down_w), local)
    waiting = list(loads)

    def work(parts):
        while waiting:
            waiting.pop().wait()
        rows = jnp.concatenate([all_ref[source, rows] for source, rows in parts], axis=0)
        gate = nn(rows, gate_w[...])
        up = nn(rows, up_w[...])
        for source, at, value in split_rows(gate, parts):
            gate_ref[source, at] = value.astype(BF)
        for source, at, value in split_rows(up, parts):
            up_ref[source, at] = value.astype(BF)
        product = (gate * jax.nn.sigmoid(gate) * up).astype(BF)
        return nn(product, down_w[...])

    total = exchange(
        normed_ref, all_ref, part, far_part, near_sum, part_in, far_in, near_in, Copies(send, recv), work
    )
    out_ref[...] = (hidden_ref[...] + total).astype(BF)


def mlp_forward(normed2, hidden, gate_w, up_w, down_w):
    return pl.pallas_call(
        mlp_forward_kernel,
        out_shape=(
            shaped(ROWS, D),
            shaped(4, ROWS, D),
            shaped(4, ROWS, QUARTER),
            shaped(4, ROWS, QUARTER),
        ),
        in_specs=[VMEM_SPEC] * 2 + [ANY_SPEC] * 3,
        scratch_shapes=EXCHANGE_SCRATCH,
        compiler_params=params(3),
        name="mlp_forward",
    )(normed2, hidden, gate_w, up_w, down_w)


def mlp_backward_kernel(
    dout_ref, gate_ref, up_ref, gate_hbm, up_hbm, down_hbm,
    dnormed_ref, all_ref, dgate_ref, dup_ref, product_ref,
    gate_w, up_w, down_w, part, far_part, near_sum, part_in, far_in, near_in, send, recv, local
):
    loads = mlp_start((gate_hbm, up_hbm, down_hbm), (gate_w, up_w, down_w), local)
    waiting = list(loads)

    def work(parts):
        while waiting:
            waiting.pop().wait()

        def stacked(ref):
            return jnp.concatenate([ref[source, rows] for source, rows in parts], axis=0)

        dproduct = nt(stacked(all_ref), down_w[...])
        gate = stacked(gate_ref).astype(F32)
        up = stacked(up_ref).astype(F32)
        s = jax.nn.sigmoid(gate)
        silu = gate * s
        product = (silu * up).astype(BF)
        dgate = (dproduct * up * (s * (1.0 + gate * (1.0 - s)))).astype(BF)
        dup = (dproduct * silu).astype(BF)
        for to, whole in ((product_ref, product), (dgate_ref, dgate), (dup_ref, dup)):
            for source, at, value in split_rows(whole, parts):
                to[source, at] = value
        return nt(dgate, gate_w[...]) + nt(dup, up_w[...])

    dnormed_ref[...] = exchange(
        dout_ref, all_ref, part, far_part, near_sum, part_in, far_in, near_in, Copies(send, recv), work
    )


def mlp_backward(dout, gate, up, gate_w, up_w, down_w):
    return pl.pallas_call(
        mlp_backward_kernel,
        out_shape=(
            shaped(ROWS, D, dtype=F32),
            shaped(4, ROWS, D),
            shaped(4, ROWS, QUARTER),
            shaped(4, ROWS, QUARTER),
            shaped(4, ROWS, QUARTER),
        ),
        in_specs=[VMEM_SPEC] * 3 + [ANY_SPEC] * 3,
        scratch_shapes=EXCHANGE_SCRATCH,
        compiler_params=params(4),
        name="mlp_backward",
    )(dout, gate, up, gate_w, up_w, down_w)


def replica_sum_kernel(
    gate, up, down, qkv, out, gate_all, up_all, down_all, qkv_all, out_all,
    qkv_low, out_low, qkv_in, out_in, send, recv, local
):
    me, mate, next_, far = replica_partners()
    to_mate, to_next = {"replica": mate}, {"replica": next_}
    core = lax.rem(me, 2)
    target, source, stays = quarter_route()
    signal([to_mate, to_next])

    @pl.when(jnp.logical_not(stays))
    def _():
        signal([target])
        greeted(3)

    @pl.when(stays)
    def _():
        greeted(2)

    copies = Copies(send, recv)
    qkv_low[...] = qkv[...].astype(BF)
    out_low[...] = out[...].astype(BF)
    across = [copies(qkv_low, qkv_in, to_next), copies(out_low, out_in, to_next)]
    across += [copies(ref, all_ref.at[me], to_next) for ref, all_ref in ((gate, gate_all), (up, up_all))]
    beside = [copies(ref, all_ref.at[me], to_mate) for ref, all_ref in ((gate, gate_all), (up, up_all))]
    own = []
    for index, (ref, all_ref) in enumerate(((gate, gate_all), (up, up_all))):
        own.append(pltpu.make_async_copy(ref, all_ref.at[me], local.at[index]))
        own[-1].start()

    @pl.when(jnp.logical_not(stays))
    def _():
        each = pltpu.make_async_remote_copy(
            src_ref=down,
            dst_ref=down_all.at[source["replica"]],
            send_sem=local.at[3],
            recv_sem=local.at[4],
            device_id=source,
            device_id_type=MESH,
        )
        each.start()
        each.wait()

    @pl.when(stays)
    def _():
        stored = pltpu.make_async_copy(down, down_all.at[me], local.at[2])
        stored.start()
        stored.wait()

    across.append(copies(down_all.at[me], down_all.at[me], to_next))
    beside.append(copies(down_all.at[me], down_all.at[me], to_mate))
    across[0].wait_recv()
    qkv_all[core] = qkv[...] + qkv_in[...].astype(F32)
    across[1].wait_recv()
    out_all[core] = out[...] + out_in[...].astype(F32)
    beside += [copies(ref.at[core], ref.at[core], to_mate) for ref in (qkv_all, out_all)]
    for came, all_ref in zip(across[2:], (gate_all, up_all, down_all)):
        came.wait_recv()
        beside.append(copies(all_ref.at[next_], all_ref.at[next_], to_mate))
    for each in beside:
        each.wait_recv()
    for each in own:
        each.wait()
    for each in across + beside:
        each.wait_send()


def replica_sum(gate, up, down, qkv, out):
    return pl.pallas_call(
        replica_sum_kernel,
        out_shape=(
            shaped(4, *gate.shape),
            shaped(4, *up.shape),
            shaped(4, *down.shape),
            shaped(2, *qkv.shape, dtype=F32),
            shaped(2, *out.shape, dtype=F32),
        ),
        scratch_shapes=[
            pltpu.VMEM(qkv.shape, BF),
            pltpu.VMEM(out.shape, BF),
            pltpu.VMEM(qkv.shape, BF),
            pltpu.VMEM(out.shape, BF),
            pltpu.SemaphoreType.DMA((13,)),
            pltpu.SemaphoreType.DMA((13,)),
            pltpu.SemaphoreType.DMA((5,)),
        ],
        compiler_params=params(5),
        name="replica_sum",
    )(gate, up, down, qkv, out)


def outputs_kernel(gate, up, down, qkv, out, gate_out, up_out, down_out, qkv_out, small_out, out_out):
    for r in range(4):
        lanes = slice(QUARTER * r, QUARTER * r + QUARTER)
        gate_out[:, lanes] = gate[r].astype(F32)
        up_out[:, lanes] = up[r].astype(F32)
        skip = 80 * r - DOWN_STARTS[r]
        down_out[80 * r : DOWN_STARTS[r] + DOWN_ROWS] = down[r, skip:].astype(F32)
    qkv_out[:32] = qkv[0]
    qkv_out[32:] = qkv[1, :24]
    small_out[...] = qkv[1, 24:, :256]
    out_out[:32] = out[0]
    out_out[32:] = out[1, :24]


def outputs(gate, up, down, qkv, out):
    return local_call(
        outputs_kernel,
        "outputs",
        (
            shaped(56, FF, dtype=F32),
            shaped(56, FF, dtype=F32),
            shaped(FF // 16, D, dtype=F32),
            shaped(56, QKV, dtype=F32),
            shaped(8, 256, dtype=F32),
            shaped(56, D, dtype=F32),
        ),
    )(gate, up, down, qkv, out)


def turn(values, cosine, sine, sign):
    width = values.shape[1]
    up = pltpu.roll(values, width - HALF, 1)
    down = pltpu.roll(values, HALF, 1)
    lane = lax.broadcasted_iota(jnp.int32, values.shape, 1)
    swapped = jnp.where(lax.rem(lane, 2 * HALF) < HALF, up, down)
    repeat = width // KV
    cosine = jnp.concatenate([cosine] * repeat, axis=1)
    sine = jnp.concatenate([sine] * repeat, axis=1)
    return values * cosine + sign * (swapped * sine)


def front_work(x_ref, w_ref, b_ref, g_ref, cos_ref, sin_ref, normed_ref, q_ref, kv_ref, copies, ready):
    z, y, along_y, along_z = grid_place()
    x = x_ref[...].astype(F32)
    inverse = lax.rsqrt(jnp.mean(x * x, axis=-1, keepdims=True) + EPSILON)
    normed = (x * inverse * g_ref[...]).astype(BF)
    normed_ref[...] = normed
    projected = nn(normed, w_ref[:, D:]) + b_ref[:, D:]
    turned = turn(projected[:, :KV], cos_ref[...], sin_ref[...], 1.0)
    kv = jnp.concatenate([turned, projected[:, KV:]], axis=1).astype(BF)
    kv_ref[0, z, y] = kv[:64]
    kv_ref[1, z, y] = kv[64:]
    ready()
    top, bottom = (slice(0, 32), slice(None)), (slice(32, 64), slice(None))
    steps = gather_both(
        y_then_z(kv_ref.at[0], *top),
        y_then_z(kv_ref.at[0], *bottom),
        z_then_y(kv_ref.at[1], *top),
        z_then_y(kv_ref.at[1], *bottom),
        copies,
    )
    next(steps)
    projected = nn(normed, w_ref[:, :D]) + b_ref[:, :D]
    q_ref[...] = turn(projected, cos_ref[...], sin_ref[...], 1.0).astype(BF)
    run(steps)


def front_kernel(x_ref, w_ref, b_ref, g_ref, cos_ref, sin_ref, normed_ref, q_ref, kv_ref, send, recv):
    z, y, along_y, along_z = grid_place()
    signal(neighbours(along_y, along_z))
    front_work(
        x_ref, w_ref, b_ref, g_ref, cos_ref, sin_ref, normed_ref, q_ref, kv_ref,
        Copies(send, recv), lambda: greeted(4)
    )


def front(x, w_qkv, b_qkv, g_attn, cosine, sine):
    return pl.pallas_call(
        front_kernel,
        out_shape=(shaped(ROWS, D), shaped(ROWS, D), shaped(2, 4, 4, 64, 2 * KV)),
        scratch_shapes=[pltpu.SemaphoreType.DMA((24,)), pltpu.SemaphoreType.DMA((24,))],
        compiler_params=params(6),
        name="front",
    )(x, w_qkv, b_qkv, g_attn, cosine, sine)


def low_lanes(rows):
    return lax.broadcasted_iota(jnp.int32, (rows, KV), 1) < KV // 2


def spread(kv_ref, start, to_ref):
    mixed = kv_ref[:, :, :, :, start : start + KV].reshape(LEN, KV)
    other = pltpu.roll(mixed.astype(F32), KV // 2, 1).astype(BF)
    low = low_lanes(LEN)
    to_ref[0] = jnp.where(low, mixed, other)
    to_ref[1] = mixed
    to_ref[2] = jnp.where(low, other, mixed)


def fill_bias(kseg_ref, bias_refs):
    first_row = 64 * lax.axis_index("group")
    for block, bias_ref in enumerate(bias_refs):
        keys = SPAN * (block + 1)
        kpos = lax.broadcasted_iota(jnp.int32, (64, keys), 1)
        qpos = SPAN * block + first_row + lax.broadcasted_iota(jnp.int32, (64, keys), 0)
        kseg = jnp.broadcast_to(kseg_ref[:, :keys], (64, keys)).astype(F32)
        qseg = jnp.sum(jnp.where(kpos == qpos, kseg, 0.0), axis=1, keepdims=True)
        bias_ref[...] = jnp.where((kpos <= qpos) & (kseg == qseg), 0.0, NEGATIVE)


def two_heads(pair):
    low = low_lanes(64)
    zero = jnp.zeros_like(pair)
    return jnp.concatenate([jnp.where(low, pair, zero), jnp.where(low, zero, pair)], axis=0)


def one_pair(stacked):
    return jnp.where(low_lanes(64), stacked[:64], stacked[64:])


def softmax(queries, keys, bias_ref):
    count = keys.shape[0]
    scores = nt(queries, keys).reshape(2, 64, count) + bias_ref[...][None]
    highest = jnp.max(scores, axis=-1, keepdims=True)
    exponent = jnp.exp(scores - highest)
    total = jnp.sum(exponent, axis=-1, keepdims=True)
    return (exponent * (1.0 / total)).reshape(2 * 64, count)


def variant_of(pair):
    return jnp.where(pair < 3, 0, jnp.where(pair == 3, 1, 2))


def attention_work(
    x_ref, q_ref, kv_ref, kseg_ref, w_ref, g_ref, context_ref, hidden_ref, normed_ref,
    keys_ref, values_ref, bias0, bias1
):
    spread(kv_ref, 0, keys_ref)
    spread(kv_ref, KV, values_ref)
    fill_bias(kseg_ref, (bias0, bias1))

    def one(pair, carry):
        variant = variant_of(pair)
        lanes = pl.ds(pl.multiple_of(pair * KV, KV), KV)
        for block, bias_ref in enumerate((bias0, bias1)):
            rows = slice(64 * block, 64 * block + 64)
            keys = pl.ds(0, SPAN * (block + 1))
            queries = two_heads(q_ref[rows, lanes] * SCALE).astype(BF)
            weights = softmax(queries, keys_ref[variant, keys], bias_ref).astype(BF)
            context = nn(weights, values_ref[variant, keys])
            context_ref[rows, lanes] = one_pair(context).astype(BF)
        return carry

    lax.fori_loop(0, PAIRS, one, 0)
    hidden = x_ref[...].astype(F32) + nn(context_ref[...], w_ref[...])
    hidden_ref[...] = hidden
    inverse = lax.rsqrt(jnp.mean(hidden * hidden, axis=-1, keepdims=True) + EPSILON)
    normed_ref[...] = (hidden * inverse * g_ref[...]).astype(BF)


ATTENTION_SCRATCH = [
    pltpu.VMEM((3, LEN, KV), BF),
    pltpu.VMEM((3, LEN, KV), BF),
    pltpu.VMEM((64, SPAN), F32),
    pltpu.VMEM((64, LEN), F32),
]


def attention(x, q, kv, kseg, w_out, g_mlp):
    return local_call(
        attention_work,
        "attention",
        (shaped(ROWS, D), shaped(ROWS, D, dtype=F32), shaped(ROWS, D)),
        ATTENTION_SCRATCH,
    )(x, q, kv, kseg, w_out, g_mlp)


def norm_backward(values, gain, grads):
    inverse = lax.rsqrt(jnp.mean(values * values, axis=-1, keepdims=True) + EPSILON)
    scaled = grads * gain
    dvalues = inverse * scaled - values * (
        inverse * inverse * inverse * jnp.mean(scaled * values, axis=-1, keepdims=True)
    )
    return dvalues, jnp.sum(grads * values * inverse, axis=0, keepdims=True)


def attention_backward_work(
    dout_ref, dnormed_ref, hidden_ref, g_ref, w_ref, q_ref, kv_ref, kseg_ref,
    dhidden_ref, dlow_ref, dq_ref, dkv_ref, dgain_ref,
    keys_ref, values_ref, bias0, bias1, dcontext_ref, dkeys, dvalues
):
    dnorm, dgain = norm_backward(hidden_ref[...], g_ref[...], dnormed_ref[...])
    dgain_ref[...] = dgain
    dhidden = dout_ref[...].astype(F32) + dnorm
    dhidden_ref[...] = dhidden
    dlow = dhidden.astype(BF)
    dlow_ref[...] = dlow
    dcontext_ref[...] = nt(dlow, w_ref[...]).astype(BF)
    spread(kv_ref, 0, keys_ref)
    spread(kv_ref, KV, values_ref)
    fill_bias(kseg_ref, (bias0, bias1))
    dkeys[...] = jnp.zeros_like(dkeys)
    dvalues[...] = jnp.zeros_like(dvalues)

    def one(pair, carry):
        variant = variant_of(pair)
        lanes = pl.ds(pl.multiple_of(pair * KV, KV), KV)
        for block, bias_ref in enumerate((bias0, bias1)):
            rows = slice(64 * block, 64 * block + 64)
            keys = pl.ds(0, SPAN * (block + 1))
            queries = two_heads(q_ref[rows, lanes] * SCALE).astype(BF)
            dcontext = two_heads(dcontext_ref[rows, lanes])
            key_rows = keys_ref[variant, keys]
            weights = softmax(queries, key_rows, bias_ref)
            dweights = nt(dcontext, values_ref[variant, keys])
            inner = jnp.sum(weights * dweights, axis=-1, keepdims=True)
            dscores = (weights * (dweights - inner)).astype(BF)
            dq_ref[rows, lanes] = one_pair(nn(dscores, key_rows)) * SCALE
            dkeys[variant, keys] += tn(dscores, queries)
            dvalues[variant, keys] += tn(weights.astype(BF), dcontext)
        return carry

    lax.fori_loop(0, PAIRS, one, 0)
    low = low_lanes(LEN)
    for start, total in ((0, dkeys), (KV, dvalues)):
        head0 = total[0] + pltpu.roll(total[0], KV // 2, 1)
        head1 = total[2] + pltpu.roll(total[2], KV // 2, 1)
        whole = (jnp.where(low, head0, head1) + total[1]).astype(BF)
        dkv_ref[:, :, :, :, start : start + KV] = whole.reshape(2, 4, 4, 64, KV)


ATTENTION_BACKWARD_OUT = (
    shaped(ROWS, D, dtype=F32),
    shaped(ROWS, D),
    shaped(ROWS, D, dtype=F32),
    shaped(2, 4, 4, 64, 2 * KV),
    shaped(1, D, dtype=F32),
)
ATTENTION_BACKWARD_SCRATCH = ATTENTION_SCRATCH + [
    pltpu.VMEM((ROWS, D), BF),
    pltpu.VMEM((3, LEN, KV), F32),
    pltpu.VMEM((3, LEN, KV), F32),
]


def attention_backward(*operands):
    return local_call(
        attention_backward_work, "attention_backward", ATTENTION_BACKWARD_OUT, ATTENTION_BACKWARD_SCRATCH
    )(*operands)


def last_kernel(*refs):
    ins, terms_in, outs, sums_out = refs[:8], refs[8:13], refs[13:18], refs[18:21]
    scratch, terms, bufs, (send, recv) = refs[21:28], refs[28:31], refs[31:-2], refs[-2:]
    z, y, along_y, along_z = grid_place()
    signal(neighbours(along_y, along_z))
    mlp_terms(*terms_in, *terms)
    greeted(4)
    steps = mlp_sums(*terms, *sums_out, bufs, Copies(send, recv))
    next(steps)
    attention_backward_work(*ins, *outs, *scratch)
    run(steps)


def last(*operands):
    return pl.pallas_call(
        last_kernel,
        out_shape=ATTENTION_BACKWARD_OUT
        + (shaped(56, QUARTER), shaped(56, QUARTER), shaped(DOWN_ROWS, D)),
        scratch_shapes=ATTENTION_BACKWARD_SCRATCH
        + [
            pltpu.VMEM((4, 4, 56, QUARTER), BF),
            pltpu.VMEM((4, 4, 56, QUARTER), BF),
            pltpu.VMEM((4, 4, DOWN_ROWS, D), BF),
        ]
        + scatter_scratch(*MLP_SUMS_SHAPES)
        + [pltpu.SemaphoreType.DMA((24,)), pltpu.SemaphoreType.DMA((24,))],
        compiler_params=params(1),
        name="last",
    )(*operands)


def rear_kernel(
    dkv_ref, dq_ref, cos_ref, sin_ref, w_ref, x_ref, g_ref, dhidden_ref,
    dprojected_ref, dinput_ref, dgain_ref, dbias_ref, *rest
):
    total, scratch, (send, recv) = rest[0], rest[1:-2], rest[-2:]
    z, y, along_y, along_z = grid_place()
    signal(neighbours(along_y, along_z))
    greeted(4)
    top, bottom = slice(0, 32), slice(32, 64)
    steps = scatter_both(
        [scatter_part(scratch, 0, lambda at: dkv_ref.at[0, :, at, top], stored_in(total, slice(0, 32)))],
        [scatter_part(scratch, 1, lambda at: dkv_ref.at[0, :, at, bottom], stored_in(total, slice(32, 64)))],
        [scatter_part(scratch, 2, lambda at: dkv_ref.at[1, at, :, top], stored_in(total, slice(64, 96)))],
        [scatter_part(scratch, 3, lambda at: dkv_ref.at[1, at, :, bottom], stored_in(total, slice(96, 128)))],
        Copies(send, recv),
    )
    next(steps)
    dquery = turn(dq_ref[...], cos_ref[...], sin_ref[...], -1.0).astype(BF)
    dprojected_ref[:, :D] = dquery
    dbias_ref[:, :D] = jnp.sum(dquery.astype(F32), axis=0, keepdims=True)
    dnormed = nt(dquery, w_ref[:, :D])
    run(steps)
    turned = turn(total[:, :KV], cos_ref[...], sin_ref[...], -1.0)
    dkv = jnp.concatenate([turned, total[:, KV:]], axis=1).astype(BF)
    dprojected_ref[:, D:] = dkv
    dbias_ref[:, D:] = jnp.sum(dkv.astype(F32), axis=0, keepdims=True)
    dnormed = dnormed + nt(dkv, w_ref[:, D:])
    dnorm, dgain = norm_backward(x_ref[...].astype(F32), g_ref[...], dnormed)
    dgain_ref[...] = dgain
    dinput_ref[...] = (dhidden_ref[...] + dnorm).astype(BF)


def rear(dkv, dq, cosine, sine, w_qkv, x, g_attn, dhidden):
    return pl.pallas_call(
        rear_kernel,
        out_shape=(shaped(ROWS, QKV), shaped(ROWS, D), shaped(1, D, dtype=F32), shaped(1, QKV, dtype=F32)),
        scratch_shapes=[pltpu.VMEM((ROWS, 2 * KV), F32)]
        + scatter_scratch(*[(32, 2 * KV)] * 4)
        + [pltpu.SemaphoreType.DMA((24,)), pltpu.SemaphoreType.DMA((24,))],
        compiler_params=params(7),
        name="rear",
    )(dkv, dq, cosine, sine, w_qkv, x, g_attn, dhidden)


def rotary(group):
    lane = np.arange(KV)
    frequency = jnp.asarray(THETA ** (-(lane % HALF) * 2.0 / (2 * HALF)), F32)
    sign = jnp.asarray(np.where(lane % (2 * HALF) < HALF, -1.0, 1.0), F32)
    row = lax.broadcasted_iota(jnp.int32, (ROWS, KV), 0)
    positions = group * 64 + lax.rem(row, 64) + SPAN * (row // 64)
    angles = positions.astype(F32) * frequency[None, :]
    return jnp.cos(angles), jnp.sin(angles) * sign[None, :]


def body(inputs, cotangent, segments, w_qkv, b_qkv, w_out, w_gate, w_up, w_down, g_attn, g_mlp):
    section = lax.axis_index("section")
    group = lax.axis_index("group")
    replica = lax.axis_index("replica")
    core = lax.rem(replica, 2)

    down_piece = lax.dynamic_slice(w_down[0], (jnp.minimum(80 * replica, 224), 0), (DOWN_ROWS, D))
    gate_piece = lax.dynamic_slice(w_gate[0], (0, replica * QUARTER), (D // 16, QUARTER))
    up_piece = lax.dynamic_slice(w_up[0], (0, replica * QUARTER), (D // 16, QUARTER))
    small = jnp.concatenate([b_qkv[0], g_attn[0], g_mlp[0]])
    small = jnp.pad(small[None], ((0, 7), (0, QKV - small.shape[0])))
    qkv_piece = lax.dynamic_slice(jnp.concatenate([w_qkv[0], small], axis=0), (32 * core, 0), (32, QKV))
    out_piece = lax.dynamic_slice(jnp.pad(w_out[0], ((0, 8), (0, 0))), (32 * core, 0), (32, D))

    cosine, sine = rotary(group)
    kseg = segments
    x_in = inputs[0].reshape(ROWS, D)
    cotangent_in = cotangent[0].reshape(ROWS, D)
    gate_w, up_w, down_w, qkv_w, out_w, bias, gain1, gain2, hidden, normed2 = first(
        gate_piece, up_piece, down_piece, qkv_piece, out_piece, x_in, cosine, sine, kseg
    )
    gate_w = gate_w.reshape(D, QUARTER)
    up_w = up_w.reshape(D, QUARTER)

    def forward(x):
        normed, q, kv = front(x, qkv_w, bias, gain1, cosine, sine)
        context, hidden, normed2 = attention(x, q, kv, kseg, out_w, gain2)
        output, normed2_all, gate, up = mlp_forward(normed2, hidden, gate_w, up_w, down_w)
        return output, (x, normed, q, kv, context, hidden, normed2_all, gate, up)

    def backward(dout, kept, finishing):
        x, normed, q, kv, context, hidden, normed2_all, gate, up = kept
        dnormed2, dout_all, dgate, dup, product = mlp_backward(dout, gate, up, gate_w, up_w, down_w)
        operands = (dout, dnormed2, hidden, gain2, out_w, q, kv, kseg)
        if finishing:
            dhidden, dlow, dq, dkv, dgain2, *grads = last(
                *operands, normed2_all, dgate, dup, product, dout_all
            )
        else:
            dhidden, dlow, dq, dkv, dgain2 = attention_backward(*operands)
            grads = ()
        dprojected, dinput, dgain1, dbias = rear(dkv, dq, cosine, sine, qkv_w, x, gain1, dhidden)
        return dinput, (grads, dlow, dprojected, dgain1, dgain2, dbias)

    relayed, *_ = mlp_forward(normed2, hidden, gate_w, up_w, down_w)
    relayed = lax.ppermute(relayed, "section", [(0, 1)])
    output, kept = forward(jnp.where(section == 0, x_in, relayed))
    returned, _ = backward(cotangent_in, kept, False)
    returned = lax.ppermute(returned, "section", [(1, 0)])
    dinput, terms = backward(jnp.where(section == 1, cotangent_in, returned), kept, True)

    x, normed, q, kv, context, hidden, normed2_all, gate, up = kept
    (grad_gate, grad_up, grad_down), dlow, dprojected, dgain1, dgain2, dbias = terms

    small = jnp.concatenate(
        [
            dbias[:, : D + KV].reshape(16, 64),
            dbias[:, D + KV :].reshape(16, 8),
            dgain1.reshape(16, 56),
            dgain2.reshape(16, 56),
        ],
        axis=1,
    )
    small = jnp.pad(small[:, None], ((0, 0), (0, 7), (0, QKV - small.shape[1])))
    grad_qkv, grad_out = qkv_scatter(normed, dprojected, small, context, dlow)
    parts = replica_sum(grad_gate, grad_up, grad_down, grad_qkv, grad_out)
    grad_gate, grad_up, grad_down, grad_qkv, small, grad_out = outputs(*parts)
    return (
        output.reshape(1, 1, 2, 64, D),
        dinput.reshape(1, 1, 2, 64, D),
        grad_qkv[None],
        small[:1, :64],
        small[:1, 64:72],
        grad_out[None],
        grad_gate[None],
        grad_up[None],
        grad_down[None],
        small[:1, 72:128],
        small[:1, 128:184],
    )


def solution(mesh):
    in_specs = (
        P("replica", None, "group", None),
        P("replica", None, "group", None),
        P("replica", None),
        P("section", "group", None),
        P("section", "group"),
        P("section", "group", None),
        P("section", "group", None),
        P("section", "group", None),
        P("section", "group", None),
        P("section", "group"),
        P("section", "group"),
    )
    out_specs = (
        P("section", "replica", None, "group", None),
        P("section", "replica", None, "group", None),
        P("section", "group", None),
        P("section", "group"),
        P("section", "group"),
        P("section", "group", None),
        P("section", "group", None),
        P("section", "group", None),
        P("section", "group", None),
        P("section", "group"),
        P("section", "group"),
    )
    return jax.shard_map(body, mesh=mesh, in_specs=in_specs, out_specs=out_specs, check_vma=False)
```

time: 1820 us -> 436 us (0.24)
  waiting for transfers between devices: 1170 us -> 10.4 us
  Pallas kernels: 0 us -> 392 us
  blocking collectives: 189 us -> 0 us
  local copies, waits for them, and re-layouts: 194 us -> 11.7 us
  matrix products: 149 us -> 0 us
  other arithmetic: 73.8 us -> 6.29 us
    unnamed x28 -> x0, waiting for transfers between devices: 925 us -> none
    pallas_call x0 -> x14, Pallas kernels: none -> 392 us  [the longest x1 79.1 us: first(): pl.pallas_call(first_kernel, out_shape=(shaped(4, 4, *gate.shape), shaped...]
    all_gather x5 -> x0, waiting for transfers between devices: 220 us -> none  [the longest x1 74 us: body(): lax.all_gather(shards[4], 'group', axis=0, tiled=True)]
    dot_general x39 -> x0, matrix products: 149 us -> none  [the longest x5 22.4 us: cross(): lax.dot_general(flatten(left_stack), flatten(right_stack), (((0,), (0,)),...]
    all_gather x7 -> x0, blocking collectives: 144 us -> none  [the longest x3 54.7 us: body(): lax.all_gather(value_rows, 'group', axis=1, tiled=True)]
    dynamic_update_slice x48 -> x0, local copies, waits for them, and re-layouts: 54.9 us -> none  [store(): lax.dynamic_update_index_in_dim(stack, value, slot_index, 0)]
    another operation x50 -> x0, local copies, waits for them, and re-layouts: 44.8 us -> none
    unnamed x97 -> x14, local copies, waits for them, and re-layouts: 33.1 us -> 1.41 us
  transfers between devices with their start and end apart: 21 -> 2, of which waited for: 17 -> 2; matrix products, arithmetic and copies ran while one was open for 7% -> 0% of each run, Pallas kernels for 0% -> 0%
where the time goes in v1:
time: 436 us; the launch traced here: 428 us
  Pallas kernels  392 us (90%)
  local copies, waits for them, and re-layouts  11.7 us (3%)
  waiting for transfers between devices  10.4 us (2%)
  other arithmetic  6.29 us (1%)
  starting transfers between devices  6.22 us (1%)
    pallas_call x1, Pallas kernels, first(): pl.pallas_call(first_kernel, out_shape=(shaped(4, 4, *gate.shape), shaped...  79.1 us
    pallas_call x2, Pallas kernels, mlp_backward(): pl.pallas_call(mlp_backward_kernel, out_shape=(shaped(ROWS, D, dtype=F32)...  65.4 us
    pallas_call x1, Pallas kernels, last(): pl.pallas_call(last_kernel, out_shape=ATTENTION_BACKWARD_OUT + (shaped(56...  51.1 us
    pallas_call x2, Pallas kernels, mlp_forward(): pl.pallas_call(mlp_forward_kernel, out_shape=(shaped(ROWS, D), shaped(4,...  44.9 us
    pallas_call x2, Pallas kernels, rear(): pl.pallas_call(rear_kernel, out_shape=(shaped(ROWS, QKV), shaped(ROWS, D)...  35 us
    pallas_call x1, Pallas kernels, qkv_scatter(): pl.pallas_call(qkv_scatter_kernel, out_shape=(shaped(32, QKV, dtype=F32),...  33.4 us
    pallas_call x1, Pallas kernels, replica_sum(): pl.pallas_call(replica_sum_kernel, out_shape=(shaped(4, *gate.shape), sha...  28.9 us
    pallas_call x1, Pallas kernels, attention_backward(): local_call(attention_backward_work, 'attention_backward', ATTENTION_BACKW...  19.7 us
  transfers between devices with their start and end apart: 2, of which 2 were waited for; matrix products, arithmetic and copies ran while one was open for 0% of the time, Pallas kernels for 0%

profile of v1, /device:TPU:1, one launch (start us, length us, event | category | flops | bytes accessed | tf_op | source)
XLA Modules:
  0.0 427.7 jit_solution(12313683442421518753)
XLA Ops:
  0.6 0.0 copy-start
  0.7 0.8 pad_maximum_fusion.1
  1.5 1.4 pad_dynamic-slice_fusion.2.out
  3.0 1.5 fusion.1.qkv
  4.4 0.0 copy-done
  4.4 0.7 dynamic-slice_bitcast_fusion.down
  5.1 1.8 dynamic-slice_bitcast_fusion.1
  7.0 1.7 sine_multiply_fusion
  8.7 79.1 %first.1 = (bf16[4,4,56,1216]{3,2,1,0:T(8,128)(2,1)}, bf16[4,4,56,1216]{3,2,1,0:T(8,128)(2,1)}, bf16[4,4,80,896]{3,2,1,0:T(8,128)(2,1)}, bf16[896,1152]{1,0:T(8,...) custom-call(bf16[56,1216]{1,0:T(8,128)(2,1)} %get-tuple-element.128., ...), custom_call_target="tpu_custom_call" | custom-call | tf_op jit(solution)/shard_map/first/pallas_call | solution.py:281
  87.8 0.0 copy-start.2
  87.8 22.2 %mlp_forward.2 = (bf16[128,896]{1,0:T(8,128)(2,1)}, bf16[4,128,896]{2,1,0:T(8,128)(2,1)}, bf16[4,128,1216]{2,1,0:T(8,128)(2,1)}, bf16[4,128,1216]{2,1,0:T(8,128)(2,1)}) custom-call(bf16[128,896]{1,0:T(8,128)(2,1)} %get-tuple-element.67.normed_ref, f32[128,896]{1,0:T(8,128)} %get-tuple-element.68.hidden_ref, bf16[896,1216]{1,0:T(8,128)(2,1)} %bitcast.24, ...), custom_call_target="tpu_custom_call" | custom-call | tf_op jit(solution)/shard_map/mlp_forward/pallas_call | solution.py:610
  110.0 4.9 %collective-permute-start = (bf16[128,896]{1,0:T(8,128)(2,1)}, bf16[128,896]{1,0:T(8,128)(2,1)S(1)}, u32[]{:S(2)}, u32[]{:S(2)}) collective-permute-start(bf16[128,896]{1,0:T(8,128)(2,1)} %get-tuple-element.72), channel_id=1, source_target_pairs={{0,64},{1,65},{2,66},{3,67},{4,68},{5,69},{6,70},{7,71},{8,72},{9,... | collective-permute-start | bytes 688136 | tf_op jit(solution)/shard_map/ppermute | solution.py:1147
  114.9 3.0 collective-permute-done
  117.9 0.0 copy-done.2
  117.9 0.7 broadcast_select_fusion.1.x_ref
  118.6 17.6 %front.1 = (bf16[128,896]{1,0:T(8,128)(2,1)}, bf16[128,896]{1,0:T(8,128)(2,1)}, bf16[2,4,4,64,256]{4,3,2,1,0:T(8,128)(2,1)}) custom-call(bf16[128,896]{1,0:T(8,128)(2,1)} %broadcast_select_fusion.1.x_ref, bf16[896,1152]{1,0:T(8,128)(2,1)} %get-tuple-element.73.w_ref, f32[1,1152]{1,0:T(1,128)} %get-tuple-element.74.b_ref, f32[1,896]{1,0:T(1,128)} %get-tuple-element.75.g_ref, ...), custom_call_target="tpu_custom_call" | custom-call | tf_op jit(solution)/shard_map/front/pallas_call | solution.py:843
  136.3 13.3 %attention.1 = (bf16[128,896]{1,0:T(8,128)(2,1)}, f32[128,896]{1,0:T(8,128)}, bf16[128,896]{1,0:T(8,128)(2,1)}) custom-call(bf16[128,896]{1,0:T(8,128)(2,1)} %broadcast_select_fusion.1.x_ref, bf16[128,896]{1,0:T(8,128)(2,1)} %get-tuple-element.76.q_ref.refs_5_, bf16[2,4,4,64,256]{4,3,2,1,0:T(8,128)(2,1)} %get-tuple-element.77.kv_ref.refs_6_, ...), custom_call_target="tpu_custom_call" | custom-call | tf_op jit(solution)/shard_map/attention/pallas_call | solution.py:935
  149.6 22.7 %mlp_forward.3 = (bf16[128,896]{1,0:T(8,128)(2,1)}, bf16[4,128,896]{2,1,0:T(8,128)(2,1)}, bf16[4,128,1216]{2,1,0:T(8,128)(2,1)}, bf16[4,128,1216]{2,1,0:T(8,128)(2,1)}) custom-call(bf16[128,896]{1,0:T(8,128)(2,1)} %get-tuple-element.80.normed_ref, f32[128,896]{1,0:T(8,128)} %get-tuple-element.81.hidden_ref.refs_2_, bf16[896,1216]{1,0:T(8,128)(2,1)} %bitcast.25, ...), custom_call_target="tpu_custom_call" | custom-call | tf_op jit(solution)/shard_map/mlp_forward/pallas_call | solution.py:610
  172.3 37.2 %mlp_backward.2 = (f32[128,896]{1,0:T(8,128)}, bf16[4,128,896]{2,1,0:T(8,128)(2,1)}, bf16[4,128,1216]{2,1,0:T(8,128)(2,1)}, bf16[4,128,1216]{2,1,0:T(8,128)(2,1)}, bf16[4,128,1216]{2,1,0:T(8,128)(2,1)}) custom-call(bf16[128,896]{1,0:T(8,128)(2,1)} %bitcast.32, bf16[4,128,1216]{2,1,0:T(8,128)(2,1)} %get-tuple-element.83.gate_ref, ...), custom_call_target="tpu_custom_call" | custom-call | tf_op jit(solution)/shard_map/mlp_backward/pallas_call | solution.py:659
  209.5 19.7 %attention_backward.1 = (f32[128,896]{1,0:T(8,128)}, bf16[128,896]{1,0:T(8,128)(2,1)}, f32[128,896]{1,0:T(8,128)}, bf16[2,4,4,64,256]{4,3,2,1,0:T(8,128)(2,1)}, f32[1,896]{1,0:T(1,128)}) custom-call(bf16[128,896]{1,0:T(8,128)(2,1)} %bitcast.33, f32[128,896]{1,0:T(8,128)} %get-tuple-element.85.dnormed_ref, f32[128,896]{1,0:T(8,128)} %get-tuple-element.81.hidden_ref.refs_2_, ...), custom_call_target="tpu_custom_call" | custom-call | tf_op jit(solution)/shard_map/attention_backward/pallas_call | solution.py:1012
  229.2 0.0 copy-start.1
  229.2 18.2 %rear.2 = (bf16[128,1152]{1,0:T(8,128)(2,1)}, bf16[128,896]{1,0:T(8,128)(2,1)}, f32[1,896]{1,0:T(1,128)}, f32[1,1152]{1,0:T(1,128)}) custom-call(bf16[2,4,4,64,256]{4,3,2,1,0:T(8,128)(2,1)} %get-tuple-element.86.dkv_ref, f32[128,896]{1,0:T(8,128)} %get-tuple-element.87.dq_ref, f32[128,128]{1,0:T(8,128)} %get-tuple-element.126.cos_ref, ...), custom_call_target="tpu_custom_call" | custom-call | tf_op jit(solution)/shard_map/rear/pallas_call | solution.py:1081
  247.4 1.3 collective-permute-start.1
  248.7 7.4 %collective-permute-done.1 = bf16[128,896]{1,0:T(8,128)(2,1)S(1)} collective-permute-done((bf16[128,896]{1,0:T(8,128)(2,1)}, bf16[128,896]{1,0:T(8,128)(2,1)S(1)}, u32[]{:S(2)}, u32[]{:S(2)}) %collective-permute-start.1) | collective-permute-done | bytes 229408 | tf_op jit(solution)/shard_map/ppermute | solution.py:1150
  256.1 0.0 copy-done.1
  256.1 0.7 broadcast_select_fusion.dout_ref.refs_0_
  256.8 28.2 %mlp_backward.3 = (f32[128,896]{1,0:T(8,128)}, bf16[4,128,896]{2,1,0:T(8,128)(2,1)}, bf16[4,128,1216]{2,1,0:T(8,128)(2,1)}, bf16[4,128,1216]{2,1,0:T(8,128)(2,1)}, bf16[4,128,1216]{2,1,0:T(8,128)(2,1)}) custom-call(bf16[128,896]{1,0:T(8,128)(2,1)} %broadcast_select_fusion.dout_ref.refs_0_, bf16[4,128,1216]{2,1,0:T(8,128)(2,1)} %get-tuple-element.83.gate_ref, ...), custom_call_target="tpu_custom_call" | custom-call | tf_op jit(solution)/shard_map/mlp_backward/pallas_call | solution.py:659
  285.0 51.1 %last.1 = (f32[128,896]{1,0:T(8,128)}, bf16[128,896]{1,0:T(8,128)(2,1)}, f32[128,896]{1,0:T(8,128)}, bf16[2,4,4,64,256]{4,3,2,1,0:T(8,128)(2,1)}, f32[1,896]{1,0...) custom-call(bf16[128,896]{1,0:T(8,128)(2,1)} %broadcast_select_fusion.dout_ref.refs_0_, ...), custom_call_target="tpu_custom_call" | custom-call | tf_op jit(solution)/shard_map/last/pallas_call | solution.py:1031
  336.1 0.0 copy-start.5
  336.1 16.7 %rear.3 = (bf16[128,1152]{1,0:T(8,128)(2,1)}, bf16[128,896]{1,0:T(8,128)(2,1)}, f32[1,896]{1,0:T(1,128)}, f32[1,1152]{1,0:T(1,128)}) custom-call(bf16[2,4,4,64,256]{4,3,2,1,0:T(8,128)(2,1)} %get-tuple-element.96.dkv_ref, f32[128,896]{1,0:T(8,128)} %get-tuple-element.97.dq_ref, f32[128,128]{1,0:T(8,128)} %get-tuple-element.126.cos_ref, ...), custom_call_target="tpu_custom_call" | custom-call | tf_op jit(solution)/shard_map/rear/pallas_call | solution.py:1081
  352.9 0.7 slice_reduce_fusion.1
  353.5 0.7 slice_reduce_fusion
  354.2 0.1 reshape.55
  354.3 0.7 reduce.2
  355.0 0.0 copy-done.5
  355.0 0.1 reshape.58
  355.1 0.1 reshape.57
  355.2 0.1 reshape.56
  355.3 0.1 pad_maximum_fusion
  355.4 0.9 pad.14.small_ref
  356.2 33.4 %qkv_scatter.1 = (f32[32,1152]{1,0:T(8,128)}, f32[32,896]{1,0:T(8,128)}) custom-call(bf16[128,896]{1,0:T(8,128)(2,1)} %get-tuple-element.103.normed_ref, bf16[128,1152]{1,0:T(8,128)(2,1)} %get-tuple-element.104.dprojected_ref, f32[16,8,1152]{2,1,0:T(8,128)} %pad.14.small_ref, bf16[128,896]{1,0:T(8,128)(2,1)} %get-tuple-element.108.context_ref, ...), custom_call_target="tpu_custom_call" | custom-call | tf_op jit(solution)/shard_map/qkv_scatter/pallas_call | solution.py:488
  389.6 28.9 %replica_sum.1 = (bf16[4,56,1216]{2,1,0:T(8,128)(2,1)}, bf16[4,56,1216]{2,1,0:T(8,128)(2,1)}, bf16[4,80,896]{2,1,0:T(8,128)(2,1)}, f32[2,32,1152]{2,1,0:T(8,128)}, f32[2,32,896]{2,1,0:T(8,128)}) custom-call(bf16[56,1216]{1,0:T(8,128)(2,1)} %get-tuple-element.100.gate, bf16[56,1216]{1,0:T(8,128)(2,1)} %get-tuple-element.101.up, ...), custom_call_target="tpu_custom_call" | custom-call | tf_op jit(solution)/shard_map/replica_sum/pallas_call | solution.py:743
  418.5 0.0 copy-start.3
  418.5 0.0 copy-start.4
  418.5 3.7 outputs.1
  422.2 1.3 slice.21
  423.4 1.2 slice.20
  424.6 1.3 fusion.4
  425.9 0.0 copy-done.3
  425.9 0.7 copy.26
  426.6 0.0 copy-done.4
  426.6 0.7 copy.27
  (6 shorter events, 0.1 us)
Async XLA Ops:
  0.6 3.8 copy-start
  87.8 30.1 %copy-start.2 = (bf16[1,2,64,896]{3,2,1,0:T(8,128)(2,1)S(1)}, bf16[1,2,64,896]{3,2,1,0:T(8,128)(2,1)}, u32[]{:S(2)}) copy-start(bf16[1,2,64,896]{3,2,1,0:T(8,128)(2,1)} %param.13) | copy-start | bytes 688132
  110.0 7.9 %collective-permute-start = (bf16[128,896]{1,0:T(8,128)(2,1)}, bf16[128,896]{1,0:T(8,128)(2,1)S(1)}, u32[]{:S(2)}, u32[]{:S(2)}) collective-permute-start(bf16[128,896]{1,0:T(8,128)(2,1)} %get-tuple-element.72), channel_id=1, source_target_pairs={{0,64},{1,65},{2,66},{3,67},{4,68},{5,69},{6,70},{7,71},{8,72},{9,... | collective-permute-start | bytes 688136 | tf_op jit(solution)/shard_map/ppermute | solution.py:1147
  229.2 26.9 %copy-start.1 = (bf16[1,2,64,896]{3,2,1,0:T(8,128)(2,1)S(1)}, bf16[1,2,64,896]{3,2,1,0:T(8,128)(2,1)}, u32[]{:S(2)}) copy-start(bf16[1,2,64,896]{3,2,1,0:T(8,128)(2,1)} %param.14) | copy-start | bytes 688132
  247.4 8.7 %collective-permute-start.1 = (bf16[128,896]{1,0:T(8,128)(2,1)}, bf16[128,896]{1,0:T(8,128)(2,1)S(1)}, u32[]{:S(2)}, u32[]{:S(2)}) collective-permute-start(bf16[128,896]{1,0:T(8,128)(2,1)} %get-tuple-element.89), channel_id=1, source_target_pairs={{64,0},{65,1},{66,2},{67,3},{68,4},{69,5},{70,6},{71,7},{72,8},{73... | collective-permute-start | bytes 688136 | tf_op jit(solution)/shard_map/ppermute | solution.py:1150
  336.1 18.9 %copy-start.5 = (f32[1,896]{1,0:T(1,128)S(1)}, f32[1,896]{1,0:T(1,128)}, u32[]{:S(2)}) copy-start(f32[1,896]{1,0:T(1,128)} %get-tuple-element.107) | copy-start | bytes 10756
  418.5 7.4 %copy-start.3 = (bf16[128,896]{1,0:T(8,128)(2,1)S(1)}, bf16[128,896]{1,0:T(8,128)(2,1)}, u32[]{:S(2)}) copy-start(bf16[128,896]{1,0:T(8,128)(2,1)} %get-tuple-element.82) | copy-start | bytes 688132
  418.5 8.1 %copy-start.4 = (bf16[128,896]{1,0:T(8,128)(2,1)S(1)}, bf16[128,896]{1,0:T(8,128)(2,1)}, u32[]{:S(2)}) copy-start(bf16[128,896]{1,0:T(8,128)(2,1)} %get-tuple-element.99) | copy-start | bytes 688132
